TPU v7x, 128 devices: a whole 4x4x4 slice. The times are simulated.
128 devices in a mesh: view: 16 (over x_lo, y, core), fsdp: 8 (over x_hi, z).
Axes of the slice: x: 4 (x_hi: 2, x_lo: 2; x = x_hi * 2 + x_lo), y: 4, z: 4, core: 2. Of those that a mesh axis runs over, the one named last changes fastest.
Arguments:
- latents: bfloat16 [8, 16, 2, 256, 1024], P('fsdp', 'view'), may hold values from -17 to 17
- w_qkv: bfloat16 [1024, 3072], P('fsdp'), may hold values from -0.1875 to 0.1875
- cycle_links: int32 [8, 16], P('fsdp'), may hold values 0 or 1
- cross_links: int32 [8, 8], P('fsdp'), may hold values 0 or 1
- d_attended: bfloat16 [8, 16, 2, 256, 1024], P('fsdp', 'view'), may hold values from -6 to 6
Outputs:
- attended: bfloat16 [8, 16, 2, 256, 1024], P('fsdp', 'view')
- d_latents: bfloat16 [8, 16, 2, 256, 1024], P('fsdp', 'view')
- d_wqkv: float32 [1024, 3072], P('fsdp')
All inputs are finite; a program needn't handle non-finite values. No bound on the sum of `cycle_links` or of `cross_links` on one device may be relied on, other than what follows from the above.
Results may differ from a plain program's by a relative error of at most 0.012.
The roundings to bfloat16 on the way count: a program that leaves them out, or rounds other values in their place, can miss the bound.
Values may be sent and summed in bfloat16 or wider, within the bound.
A program may use at most 128 MiB of HBM per device.

v0:
```python
import jax
import jax.numpy as jnp
from jax import lax
from jax.sharding import PartitionSpec as P

HEAD_DIM = 64


score_scale = 0.125


def passed_along(shard, axis, by):
    peers = lax.axis_size(axis)
    return lax.ppermute(shard, axis, [(i, (i + by) % peers) for i in range(peers)])


def local(latents, w_qkv, cycle_links, cross_links, d_attended):
    samples = latents.shape[2]
    tokens_view = latents.shape[3]
    model_width = latents.shape[4]
    flat_rows = latents.reshape(samples * tokens_view, model_width)
    weights = lax.all_gather(w_qkv, "fsdp", axis=0, tiled=True)
    projected = jnp.dot(flat_rows, weights, preferred_element_type=jnp.float32).astype(jnp.bfloat16)
    projected = projected.reshape(samples, tokens_view, 3 * model_width)
    queries = projected[:, :, :model_width]
    own_kv = projected[:, :, model_width:]
    grad_attended = d_attended[0, 0]
    view_total = lax.axis_size("view")
    half_cycle = view_total // 2
    view_pos = lax.axis_index("view")
    cycle_row = cycle_links[0]
    cycle_own = lax.dynamic_index_in_dim(cycle_row, view_pos, 0, keepdims=False)
    cycle_back = lax.dynamic_index_in_dim(
        cycle_row, (view_pos + view_total - 2) % view_total, 0, keepdims=False
    )
    cross_own = lax.dynamic_index_in_dim(cross_links[0], view_pos % half_cycle, 0, keepdims=False)
    offsets = (1, -1, 2, -2, half_cycle)
    blocks = [own_kv]
    for offset in offsets:
        blocks.append(passed_along(own_kv, "view", offset))
    unit = jnp.ones((), jnp.float32)
    slot_mask = jnp.stack(
        [
            unit,
            unit,
            unit,
            cycle_back.astype(jnp.float32),
            cycle_own.astype(jnp.float32),
            cross_own.astype(jnp.float32),
        ]
    )
    key_mask = jnp.repeat(slot_mask, tokens_view)
    head_pair = 128
    pair_count = head_pair // HEAD_DIM

    def take(source, column):
        return lax.dynamic_slice_in_dim(source, column, head_pair, 2)

    def group_step(block_index, carry):
        attended, grad_query, own_grads, neighbour_grads = carry
        column = block_index * head_pair
        query_part = take(queries, column).reshape(samples, tokens_view, pair_count, HEAD_DIM)
        key_part = jnp.concatenate([take(block, column) for block in blocks], axis=1)
        key_part = key_part.reshape(samples, 6 * tokens_view, pair_count, HEAD_DIM)
        value_part = jnp.concatenate(
            [take(block, model_width + column) for block in blocks], axis=1
        )
        value_part = value_part.reshape(samples, 6 * tokens_view, pair_count, HEAD_DIM)
        grad_out = take(grad_attended, column).reshape(samples, tokens_view, pair_count, HEAD_DIM)
        scores = (
            jnp.einsum("bqhd,bkhd->bhqk", query_part, key_part, preferred_element_type=jnp.float32)
            * score_scale
        )
        masked = jnp.where(key_mask > 0.5, scores, -1e30)
        row_peak = jnp.max(masked, axis=-1, keepdims=True)
        weights_raw = jnp.exp(masked - row_peak)
        denominator = jnp.sum(weights_raw, axis=-1, keepdims=True)
        probabilities = weights_raw / denominator
        rounded_probs = probabilities.astype(jnp.bfloat16)
        output = jnp.einsum(
            "bhqk,bkhd->bqhd", rounded_probs, value_part, preferred_element_type=jnp.float32
        )
        row_delta = jnp.transpose(
            jnp.sum(grad_out.astype(jnp.float32) * output, axis=-1), (0, 2, 1)
        )[..., None]
        grad_probs = jnp.einsum(
            "bqhd,bkhd->bhqk", grad_out, value_part, preferred_element_type=jnp.float32
        )
        grad_scores = (probabilities * (grad_probs - row_delta) * score_scale).astype(jnp.bfloat16)
        grad_q = jnp.einsum(
            "bhqk,bkhd->bqhd", grad_scores, key_part, preferred_element_type=jnp.float32
        )
        grad_k = jnp.einsum(
            "bhqk,bqhd->bkhd", grad_scores, query_part, preferred_element_type=jnp.float32
        )
        grad_v = jnp.einsum(
            "bhqk,bqhd->bkhd", rounded_probs, grad_out, preferred_element_type=jnp.float32
        )
        grad_q = grad_q.reshape(samples, tokens_view, head_pair)
        grad_k = grad_k.reshape(samples, 6 * tokens_view, head_pair)
        grad_v = grad_v.reshape(samples, 6 * tokens_view, head_pair)
        attended = lax.dynamic_update_slice_in_dim(
            attended,
            output.astype(jnp.bfloat16).reshape(samples, tokens_view, head_pair),
            column,
            2,
        )
        grad_query = lax.dynamic_update_slice_in_dim(grad_query, grad_q, column, 2)
        own_grads = lax.dynamic_update_slice_in_dim(own_grads, grad_k[:, :tokens_view], column, 2)
        own_grads = lax.dynamic_update_slice_in_dim(
            own_grads, grad_v[:, :tokens_view], model_width + column, 2
        )
        far_k = jnp.transpose(
            grad_k[:, tokens_view:].reshape(samples, 5, tokens_view, head_pair), (1, 0, 2, 3)
        )
        far_v = jnp.transpose(
            grad_v[:, tokens_view:].reshape(samples, 5, tokens_view, head_pair), (1, 0, 2, 3)
        )
        neighbour_grads = lax.dynamic_update_slice_in_dim(
            neighbour_grads, far_k.astype(jnp.bfloat16), column, 3
        )
        neighbour_grads = lax.dynamic_update_slice_in_dim(
            neighbour_grads, far_v.astype(jnp.bfloat16), model_width + column, 3
        )
        return (attended, grad_query, own_grads, neighbour_grads)

    initial = (
        jnp.zeros((samples, tokens_view, model_width), jnp.bfloat16),
        jnp.zeros((samples, tokens_view, model_width), jnp.float32),
        jnp.zeros((samples, tokens_view, 2 * model_width), jnp.float32),
        jnp.zeros((5, samples, tokens_view, 2 * model_width), jnp.bfloat16),
    )
    attended, grad_query, own_grads, neighbour_grads = lax.fori_loop(
        0, model_width // head_pair, group_step, initial
    )
    kv_grads = own_grads
    for neighbour, offset in enumerate(offsets):
        returned = passed_along(neighbour_grads[neighbour], "view", -offset)
        kv_grads = kv_grads + returned.astype(jnp.float32)
    grad_proj = (
        jnp.concatenate([grad_query, kv_grads], axis=-1)
        .astype(jnp.bfloat16)
        .reshape(-1, 3 * model_width)
    )
    grad_latents = jnp.einsum(
        "nc,dc->nd", grad_proj, weights, preferred_element_type=jnp.float32
    ).astype(jnp.bfloat16)
    grad_latents = grad_latents.reshape(latents.shape)
    partial_rows = lax.psum_scatter(
        lax.dot_general(
            flat_rows, grad_proj, (((0,), (0,)), ((), ())), preferred_element_type=jnp.float32
        ),
        "fsdp",
        scatter_dimension=0,
        tiled=True,
    )
    grad_weight = lax.psum(partial_rows, "view")
    return (attended[None, None], grad_latents, grad_weight)


def solution(mesh):
    placed = (
        P("fsdp", "view", None, None, None),
        P("fsdp", None),
        P("fsdp", None),
        P("fsdp", None),
        P("fsdp", "view", None, None, None),
    )
    return jax.shard_map(
        local,
        mesh=mesh,
        in_specs=placed,
        out_specs=(
            P("fsdp", "view", None, None, None),
            P("fsdp", "view", None, None, None),
            P("fsdp", None),
        ),
        check_vma=False,
    )
```

profile of v0, /device:TPU:1, one launch (start us, length us, event | category | flops | bytes accessed | tf_op | source)
XLA Modules:
  0.0 949.8 jit_solution(3196945474688286412)
XLA Ops:
  8.0 94.3 %all-gather.2.cloned.1.call-done = bf16[1024,3072]{1,0:T(8,128)(2,1)} async-done(((bf16[128,3072]{1,0:T(8,128)(2,1)}), bf16[1024,3072]{1,0:T(8,128)(2,1)}) %all-gather.2.cloned.1.call-update) | async-done | bytes 6291472 | tf_op jit(solution)/shard_map/all_gather | solution.py:22
  102.2 6.4 convolution_convert_fusion
  110.5 2.5 copy.35
  113.2 3.4 collective-permute-start.3
  123.8 2.3 slice.79
  126.1 33.2 %collective-permute-done.4 = bf16[2,256,2048]{1,2,0:T(8,128)(2,1)} collective-permute-done((bf16[2,256,2048]{1,2,0:T(8,128)(2,1)}, bf16[2,256,2048]{1,2,0:T(8,128)(2,1)}, u32[]{:S(2)}, u32[]{:S(2)}) %collective-permute-start.4) | collective-permute-done | bytes 2097184 | tf_op jit(solution)/shard_map/ppermute | solution.py:14
  159.3 43.0 %collective-permute-done.3 = bf16[2,256,2048]{1,2,0:T(8,128)(2,1)} collective-permute-done((bf16[2,256,2048]{1,2,0:T(8,128)(2,1)}, bf16[2,256,2048]{1,2,0:T(8,128)(2,1)}, u32[]{:S(2)}, u32[]{:S(2)}) %collective-permute-start.3) | collective-permute-done | bytes 2097184 | tf_op jit(solution)/shard_map/ppermute | solution.py:14
  202.3 4.1 collective-permute-done.2
  208.7 2.3 broadcast_in_dim.51
  211.0 5.4 broadcast_in_dim.52
  216.4 292.3 %while.22 = (s32[]{:T(128)}, bf16[2,256,1024]{2,1,0:T(8,128)(2,1)}, bf16[2,256,1024]{2,1,0:T(8,128)(2,1)}, f32[2,256,2048]{1,2,0:T(8,128)}, bf16[5,2,256,2048]{3...) while((s32[]{:T(128)}, bf16[2,256,1024]{2,1,0:T(8,128)(2,1)}, ...), condition=%wide.region_4.5_spmd.clone, body=%wide.region_0.4_spmd.clone.sunk | while | flops 1225525248 | bytes 87604792 | solution.py:133
  223.5 4.6 fusion.67
  228.2 3.8 fusion.68
  231.9 2.6 multiply_reduce_fusion.2
  260.0 4.6 fusion.67
  264.7 3.8 fusion.68
  268.4 2.6 multiply_reduce_fusion.2
  296.6 4.6 fusion.67
  301.2 3.8 fusion.68
  305.0 2.6 multiply_reduce_fusion.2
  333.2 4.6 fusion.67
  337.8 3.8 fusion.68
  341.6 2.6 multiply_reduce_fusion.2
  369.7 4.6 fusion.67
  374.4 3.8 fusion.68
  378.1 2.6 multiply_reduce_fusion.2
  406.3 4.6 fusion.67
  410.9 3.8 fusion.68
  414.7 2.6 multiply_reduce_fusion.2
  442.8 4.6 fusion.67
  447.4 3.8 fusion.68
  451.2 2.6 multiply_reduce_fusion.2
  479.3 4.6 fusion.67
  483.9 3.8 fusion.68
  487.7 2.6 multiply_reduce_fusion.2
  508.6 7.5 slice_bitcast_fusion.4
  516.1 24.5 %collective-permute-start.5 = (bf16[2,256,2048]{2,1,0:T(8,128)(2,1)}, bf16[2,256,2048]{2,1,0:T(8,128)(2,1)}, u32[]{:S(2)}, u32[]{:S(2)}) collective-permute-start(bf16[2,256,2048]{2,1,0:T(8,128)(2,1)} %get-tuple-element.424), channel_id=1, source_target_pairs={{0,120},{8,0},{16,8},{24,16},{32,24},{40,32},{48,40},{56,48},{64,5... | collective-permute-start | bytes 6291464 | tf_op jit(solution)/shard_map/ppermute | solution.py:14
  540.9 3.6 collective-permute-start.7
  544.5 5.4 copy.25
  549.9 38.7 %collective-permute-done.9 = bf16[2,256,2048]{2,1,0:T(8,128)(2,1)} collective-permute-done((bf16[2,256,2048]{2,1,0:T(8,128)(2,1)}, bf16[2,256,2048]{2,1,0:T(8,128)(2,1)}, u32[]{:S(2)}, u32[]{:S(2)}) %collective-permute-start.9) | collective-permute-done | bytes 2097184 | tf_op jit(solution)/shard_map/ppermute | solution.py:14
  588.6 22.7 %collective-permute-done.8 = bf16[2,256,2048]{2,1,0:T(8,128)(2,1)} collective-permute-done((bf16[2,256,2048]{2,1,0:T(8,128)(2,1)}, bf16[2,256,2048]{2,1,0:T(8,128)(2,1)}, u32[]{:S(2)}, u32[]{:S(2)}) %collective-permute-start.8) | collective-permute-done | bytes 2097184 | tf_op jit(solution)/shard_map/ppermute | solution.py:14
  611.2 20.4 %collective-permute-done.7 = bf16[2,256,2048]{2,1,0:T(8,128)(2,1)} collective-permute-done((bf16[2,256,2048]{2,1,0:T(8,128)(2,1)}, bf16[2,256,2048]{2,1,0:T(8,128)(2,1)}, u32[]{:S(2)}, u32[]{:S(2)}) %collective-permute-start.7) | collective-permute-done | bytes 2097184 | tf_op jit(solution)/shard_map/ppermute | solution.py:14
  631.6 7.8 add_convert_fusion
  639.4 6.6 convolution_bitcast_fusion.1
  646.0 172.2 %reduce-scatter.2.cloned.1.call-done = f32[128,3072]{0,1:T(8,128)} async-done(((f32[1024,3072]{0,1:T(8,128)}), f32[128,3072]{0,1:T(8,128)}) %reduce-scatter.2.cloned.1.call-update) | async-done | bytes 1572880 | tf_op jit(solution)/shard_map/reduce_scatter | solution.py:149
  818.2 7.5 fusion.13
  825.7 114.5 %all-reduce.2.cloned.1.call-done = f32[128,3072]{0,1:T(8,128)} async-done(((f32[128,3072]{0,1:T(8,128)}), f32[128,3072]{0,1:T(8,128)}) %all-reduce.2.cloned.1.call-update) | async-done | bytes 1572880 | tf_op jit(solution)/shard_map/psum | solution.py:157
  940.2 3.0 copy.30
  (363 shorter events, 214.3 us)
Async XLA Ops:
  7.2 95.1 %copy-start = (bf16[1,1,2,256,1024]{4,3,2,1,0:T(8,128)(2,1)S(1)}, bf16[1,1,2,256,1024]{4,3,2,1,0:T(8,128)(2,1)}, u32[]{:S(2)}) copy-start(bf16[1,1,2,256,1024]{4,3,2,1,0:T(8,128)(2,1)} %param.7) | copy-start | bytes 3145732
  7.2 95.0 %all-gather.2.cloned.1.call-start = ((), (), s32[]{:S(2)}) async-start(), calls=%async_computation.1 | async-start | bytes 7077888 | tf_op jit(solution)/shard_map/all_gather | solution.py:22
  7.9 810.3 %reduce-scatter.2.cloned.1.call-start = ((), (), s32[]{:S(2)}) async-start(), calls=%async_computation.2 | async-start | bytes 14155776 | tf_op jit(solution)/shard_map/reduce_scatter | solution.py:149
  110.4 7.9 copy-start.8
  110.4 12.1 %copy-start.9 = (s32[1,8]{1,0:T(1,128)S(1)}, s32[1,8]{1,0:T(1,128)}, u32[]{:S(2)}) copy-start(s32[1,8]{1,0:T(1,128)} %param.10) | copy-start | bytes 100
  113.0 46.4 %collective-permute-start.4 = (bf16[2,256,2048]{1,2,0:T(8,128)(2,1)}, bf16[2,256,2048]{1,2,0:T(8,128)(2,1)}, u32[]{:S(2)}, u32[]{:S(2)}) collective-permute-start(bf16[2,256,2048]{1,2,0:T(8,128)(2,1)} %copy.35), channel_id=1, source_target_pairs={{0,64},{8,72},{16,80},{24,88},{32,96},{40,104},{48,112},{56,120},{... | collective-permute-start | bytes 6291464 | tf_op jit(solution)/shard_map/ppermute | solution.py:14
  113.2 89.1 %collective-permute-start.3 = (bf16[2,256,2048]{1,2,0:T(8,128)(2,1)}, bf16[2,256,2048]{1,2,0:T(8,128)(2,1)}, u32[]{:S(2)}, u32[]{:S(2)}) collective-permute-start(bf16[2,256,2048]{1,2,0:T(8,128)(2,1)} %copy.35), channel_id=1, source_target_pairs={{0,112},{8,120},{16,0},{24,8},{32,16},{40,24},{48,32},{56,40},{64,... | collective-permute-start | bytes 6291464 | tf_op jit(solution)/shard_map/ppermute | solution.py:14
  116.6 89.8 %collective-permute-start.2 = (bf16[2,256,2048]{1,2,0:T(8,128)(2,1)}, bf16[2,256,2048]{1,2,0:T(8,128)(2,1)}, u32[]{:S(2)}, u32[]{:S(2)}) collective-permute-start(bf16[2,256,2048]{1,2,0:T(8,128)(2,1)} %copy.35), channel_id=1, source_target_pairs={{0,16},{8,24},{16,32},{24,40},{32,48},{40,56},{48,64},{56,72},{64,... | collective-permute-start | bytes 6291464 | tf_op jit(solution)/shard_map/ppermute | solution.py:14
  116.6 89.8 %collective-permute-start.1 = (bf16[2,256,2048]{1,2,0:T(8,128)(2,1)}, bf16[2,256,2048]{1,2,0:T(8,128)(2,1)}, u32[]{:S(2)}, u32[]{:S(2)}) collective-permute-start(bf16[2,256,2048]{1,2,0:T(8,128)(2,1)} %copy.35), channel_id=1, source_target_pairs={{0,120},{8,0},{16,8},{24,16},{32,24},{40,32},{48,40},{56,48},{64,5... | collective-permute-start | bytes 6291464 | tf_op jit(solution)/shard_map/ppermute | solution.py:14
  118.2 88.2 %collective-permute-start = (bf16[2,256,2048]{1,2,0:T(8,128)(2,1)}, bf16[2,256,2048]{1,2,0:T(8,128)(2,1)}, u32[]{:S(2)}, u32[]{:S(2)}) collective-permute-start(bf16[2,256,2048]{1,2,0:T(8,128)(2,1)} %copy.35), channel_id=1, source_target_pairs={{0,8},{8,16},{16,24},{24,32},{32,40},{40,48},{48,56},{56,64},{64,7... | collective-permute-start | bytes 6291464 | tf_op jit(solution)/shard_map/ppermute | solution.py:14
  223.5 8.4 copy-start.2
  228.2 7.1 slice-start
  228.2 7.1 slice-start.1
  260.0 8.4 copy-start.2
  264.7 7.1 slice-start
  264.7 7.1 slice-start.1
  284.3 4.1 copy-start.1
  296.6 8.4 copy-start.2
  301.2 7.1 slice-start
  301.2 7.1 slice-start.1
  320.9 4.1 copy-start.1
  333.2 8.4 copy-start.2
  337.8 7.1 slice-start
  337.8 7.1 slice-start.1
  357.5 4.1 copy-start.1
  369.7 8.4 copy-start.2
  374.4 7.1 slice-start
  374.4 7.1 slice-start.1
  394.0 4.1 copy-start.1
  406.2 8.4 copy-start.2
  410.9 7.1 slice-start
  410.9 7.1 slice-start.1
  430.6 4.1 copy-start.1
  442.8 8.4 copy-start.2
  447.4 7.1 slice-start
  447.4 7.1 slice-start.1
  467.1 4.1 copy-start.1
  479.3 8.4 copy-start.2
  483.9 7.1 slice-start
  483.9 7.1 slice-start.1
  503.6 4.1 copy-start.1
  516.1 33.7 %collective-permute-start.5 = (bf16[2,256,2048]{2,1,0:T(8,128)(2,1)}, bf16[2,256,2048]{2,1,0:T(8,128)(2,1)}, u32[]{:S(2)}, u32[]{:S(2)}) collective-permute-start(bf16[2,256,2048]{2,1,0:T(8,128)(2,1)} %get-tuple-element.424), channel_id=1, source_target_pairs={{0,120},{8,0},{16,8},{24,16},{32,24},{40,32},{48,40},{56,48},{64,5... | collective-permute-start | bytes 6291464 | tf_op jit(solution)/shard_map/ppermute | solution.py:14
  540.6 48.0 %collective-permute-start.9 = (bf16[2,256,2048]{2,1,0:T(8,128)(2,1)}, bf16[2,256,2048]{2,1,0:T(8,128)(2,1)}, u32[]{:S(2)}, u32[]{:S(2)}) collective-permute-start(bf16[2,256,2048]{2,1,0:T(8,128)(2,1)} %get-tuple-element.425), channel_id=1, source_target_pairs={{0,64},{8,72},{16,80},{24,88},{32,96},{40,104},{48,112},{56,120},{... | collective-permute-start | bytes 6291464 | tf_op jit(solution)/shard_map/ppermute | solution.py:14
  540.9 70.3 %collective-permute-start.8 = (bf16[2,256,2048]{2,1,0:T(8,128)(2,1)}, bf16[2,256,2048]{2,1,0:T(8,128)(2,1)}, u32[]{:S(2)}, u32[]{:S(2)}) collective-permute-start(bf16[2,256,2048]{2,1,0:T(8,128)(2,1)} %get-tuple-element.426), channel_id=1, source_target_pairs={{0,16},{8,24},{16,32},{24,40},{32,48},{40,56},{48,64},{56,72},{64,... | collective-permute-start | bytes 6291464 | tf_op jit(solution)/shard_map/ppermute | solution.py:14
  540.9 90.7 %collective-permute-start.7 = (bf16[2,256,2048]{2,1,0:T(8,128)(2,1)}, bf16[2,256,2048]{2,1,0:T(8,128)(2,1)}, u32[]{:S(2)}, u32[]{:S(2)}) collective-permute-start(bf16[2,256,2048]{2,1,0:T(8,128)(2,1)} %get-tuple-element.427), channel_id=1, source_target_pairs={{0,112},{8,120},{16,0},{24,8},{32,16},{40,24},{48,32},{56,40},{64,... | collective-permute-start | bytes 6291464 | tf_op jit(solution)/shard_map/ppermute | solution.py:14
  544.5 87.1 %collective-permute-start.6 = (bf16[2,256,2048]{2,1,0:T(8,128)(2,1)S(1)}, bf16[2,256,2048]{2,1,0:T(8,128)(2,1)}, u32[]{:S(2)}, u32[]{:S(2)}) collective-permute-start(bf16[2,256,2048]{2,1,0:T(8,128)(2,1)S(1)} %get-tuple-element.428), channel_id=1, source_target_pairs={{0,8},{8,16},{16,24},{24,32},{32,40},{40,48},{48,56},{56,64},{64,7... | collective-permute-start | bytes 6291464 | tf_op jit(solution)/shard_map/ppermute | solution.py:14
  549.9 89.5 %copy-start.7 = (bf16[2,256,1024]{2,1,0:T(8,128)(2,1)S(1)}, bf16[2,256,1024]{2,1,0:T(8,128)(2,1)}, u32[]{:S(2)}) copy-start(bf16[2,256,1024]{2,1,0:T(8,128)(2,1)} %get-tuple-element.337) | copy-start | bytes 3145732
  646.0 294.3 %all-reduce.2.cloned.1.call-start = ((), (), s32[]{:S(2)}) async-start(), calls=%async_computation.3 | async-start | bytes 3145728 | tf_op jit(solution)/shard_map/psum | solution.py:157
  (26 other events, 44.7 us)
Sparse Core Ops, SparseCore 0:
  10.3 91.8 all-gather.1
  646.1 172.0 reduce-scatter.1
  820.7 119.4 all-reduce.1
where the time goes:
time: 953 us; the launch traced here: 950 us
  waiting for transfers between devices  544 us (57%)
  local copies, waits for them, and re-layouts  193 us (20%)
  matrix products  125 us (13%)
  other arithmetic  38.5 us (4%)
  starting transfers between devices  33.8 us (4%)
  between operations  15.1 us (2%)
    reduce_scatter x1, waiting for transfers between devices, local(): lax.psum_scatter(lax.dot_general(flat_rows, grad_proj, (((0,), (0,)), (()...  172 us
    ppermute x10, waiting for transfers between devices, passed_along(): lax.ppermute(shard, axis, [(i, (i + by) % peers) for i in range(peers)])  162 us
    psum x1, waiting for transfers between devices, local(): grad_weight = lax.psum(partial_rows, 'view')  114 us
    all_gather x1, waiting for transfers between devices, local(): weights = lax.all_gather(w_qkv, 'fsdp', axis=0, tiled=True)  94.3 us
    while x168, local copies, waits for them, and re-layouts  72.5 us
    sub x8, matrix products, group_step(): weights_raw = jnp.exp(masked - row_peak)  37.1 us
    ppermute x10, starting transfers between devices, passed_along(): lax.ppermute(shard, axis, [(i, (i + by) % peers) for i in range(peers)])  33.7 us
    convert_element_type x8, other arithmetic, group_step(): rounded_probs = probabilities.astype(jnp.bfloat16)  30.1 us
  transfers between devices with their start and end apart: 13, of which 9 were waited for; matrix products, arithmetic and copies ran while one was open for 2% of the time, Pallas kernels for 0%

commit v1 on v0

v1 whole, which is shorter than its diff:
```python
import functools

import jax
import jax.numpy as jnp
from jax import lax
from jax.experimental import pallas as pl
from jax.experimental.pallas import tpu as pltpu
from jax.sharding import PartitionSpec as P

BF, F32 = jnp.bfloat16, jnp.float32
MESH = pl.DeviceIdType.MESH
TOK = 256
LOG2E = 1.4426950408889634
SCALE = 0.125
NT = (((1,), (1,)), ((), ()))
NN = (((1,), (0,)), ((), ()))
TN = (((0,), (0,)), ((), ()))
VMEM_LIMIT = 60 * 2**20


class Place:
    def __init__(self):
        v, f = lax.axis_index("view"), lax.axis_index("fsdp")
        self.view, self.fsdp = v, f
        self.ys, self.zs = 4, 4
        self.core = v % 2
        self.y = (v // 2) % 4
        self.x_lo = v // 8
        self.z = f % 4
        self.x_hi = f // 4
        column = self.x_lo * 8 + self.core

        def at(view, fsdp):
            return {"view": view, "fsdp": fsdp}

        self.up = at(column + 2 * ((self.y + 1) % 4), f)
        self.down = at(column + 2 * ((self.y + 3) % 4), f)
        self.over = at(column + 2 * ((self.y + 2) % 4), f)
        self.pair = at((v + 8) % 16, f)
        self.mate = at(v + 1 - 2 * self.core, f)
        self.f_up = self.x_hi * 4 + (self.z + 1) % 4
        self.f_down = self.x_hi * 4 + (self.z + 3) % 4
        self.f_far = self.x_hi * 4 + (self.z + 2) % 4
        self.f_outer = (f + 4) % 8
        self.z_up = at(v, self.f_up)
        self.z_down = at(v, self.f_down)
        self.outer = at((v + 8) % 16, self.f_outer)


def greet(devices):
    barrier = pltpu.get_barrier_semaphore()
    for device in devices:
        pl.semaphore_signal(barrier, inc=1, device_id=device, device_id_type=MESH)
    pl.semaphore_wait(barrier, len(devices))


class Mail:
    def __init__(self, send, recv):
        self.send, self.recv, self.made, self.sent = send, recv, 0, []

    def copy(self, src, dst, to):
        i = self.made
        self.made += 1
        made = self.again(i, src, dst, to)
        self.sent.append(made)
        return made

    def again(self, i, src, dst, to):
        return pltpu.make_async_remote_copy(
            src_ref=src, dst_ref=dst, send_sem=self.send.at[i], recv_sem=self.recv.at[i],
            device_id=to, device_id_type=MESH)

    def finish(self):
        for copy in self.sent:
            copy.wait_send()


def at(start, size):
    return pl.ds(pl.multiple_of(start, size), size)


def dot(a, b, dims=NN):
    return lax.dot_general(a, b, dims, preferred_element_type=F32)


def gather_kernel(lat_ref, w_ref, g_ref, lat_all, w_all, g_all, local, send, recv):
    me = Place()
    c = me.core
    rows = w_ref.shape[0]
    half = w_ref.shape[1] // 6
    samples, toks = lat_ref.shape[0], lat_ref.shape[1]
    chunks = [(s, pl.ds(t * (toks // 2), toks // 2)) for s in range(samples) for t in range(2)]
    own_block, other_block = 3 + c, 4 - c
    locals_ = []
    for k in range(3):
        locals_.append(pltpu.make_async_copy(
            w_ref.at[:, pl.ds(pl.multiple_of((2 * k + c) * half, half), half)],
            w_all.at[pl.ds(pl.multiple_of(me.fsdp * rows, rows), rows), pl.ds(k * half, half)],
            local.at[k]))
    for s in range(samples):
        locals_.append(pltpu.make_async_copy(lat_ref.at[s], lat_all.at[s, own_block], local.at[3 + s]))
        locals_.append(pltpu.make_async_copy(
            g_ref.at[s, :, pl.ds(pl.multiple_of(c * half, half), half)],
            g_all.at[s, pl.ds(pl.multiple_of(c * toks, toks), toks), :], local.at[5 + s]))
    for copy in locals_:
        copy.start()
    greet((me.up, me.down, me.pair, me.mate, me.z_up, me.z_down, me.outer))

    mail = Mail(send, recv)
    remote = mail.copy

    def block(b, chunk):
        s, t = chunk
        return lat_all.at[s, b, t]

    def shard(f, part=None):
        if part is None:
            return w_all.at[pl.ds(pl.multiple_of(f * rows, rows), rows)]
        return w_all.at[pl.ds(pl.multiple_of(f * rows + part * (rows // 2), rows // 2), rows // 2)]

    n = range(len(chunks))
    mine = [lat_ref.at[s, t] for s, t in chunks]
    to_pair = [remote(mine[i], block(7 * c, chunks[i]), me.pair) for i in n]
    to_mate = [remote(mine[i], block(own_block, chunks[i]), me.mate) for i in n]
    up = [remote(mine[i], block(1 + c, chunks[i]), me.up) for i in n]
    down = [remote(mine[i], block(5 + c, chunks[i]), me.down) for i in n]
    up_far = [mail.again(2 * len(chunks) + i, block(7 * c, chunks[i]), block(1 + c, chunks[i]), me.up) for i in n]
    down_far = [mail.again(3 * len(chunks) + i, block(7 * c, chunks[i]), block(5 + c, chunks[i]), me.down) for i in n]
    relay_pair = [remote(block(7 * c, chunks[i]), block(7 * c, chunks[i]), me.mate) for i in n]
    relay_up = [remote(block(1 + c, chunks[i]), block(1 + c, chunks[i]), me.mate) for i in n]
    relay_down = [remote(block(5 + c, chunks[i]), block(5 + c, chunks[i]), me.mate) for i in n]
    g_mate = [remote(
        g_ref.at[s, :, pl.ds(pl.multiple_of((1 - c) * half, half), half)],
        g_all.at[s, pl.ds(pl.multiple_of(c * toks, toks), toks), :], me.mate) for s in range(samples)]

    first, last = me.y == 0, me.y == me.ys - 1
    f0, fz_up, fz_down, f_out = me.fsdp, me.f_up, me.f_down, me.f_outer
    w_up = remote(shard(f0), shard(f0), me.z_up)
    w_down = remote(shard(f0), shard(f0), me.z_down)
    w_out = remote(shard(f0), shard(f0), me.outer)
    w_up2 = remote(shard(fz_down, 0), shard(fz_down, 0), me.z_up)
    w_down2 = remote(shard(fz_up, 1), shard(fz_up, 1), me.z_down)
    o_up = remote(shard(f_out), shard(f_out), me.z_up)
    o_down = remote(shard(f_out), shard(f_out), me.z_down)
    far = me.f_far
    o_far = [remote(shard(far, part), shard(far, part), me.outer) for part in range(2)]

    for i in n:
        to_pair[i].start()
        if i == 0:
            for copy in locals_[:3]:
                copy.wait()
            w_up.start()
            w_down.start()
            w_out.start()

        @pl.when(jnp.logical_not(last))
        def _(i=i):
            up[i].start()

        @pl.when(jnp.logical_not(first))
        def _(i=i):
            down[i].start()
    for i in n:
        to_mate[i].start()
    for copy in g_mate:
        copy.start()

    def pair_in(i):
        to_pair[i].wait_recv()

        @pl.when(last)
        def _():
            up_far[i].start()

        @pl.when(first)
        def _():
            down_far[i].start()
        relay_pair[i].start()

    def y_in(i):
        up[i].wait_recv()
        relay_up[i].start()
        down[i].wait_recv()
        relay_down[i].start()

    pair_in(0)
    w_up.wait_recv()
    w_up2.start()
    w_down.wait_recv()
    w_down2.start()
    w_out.wait_recv()
    o_up.start()
    o_down.start()
    pair_in(1)
    y_in(0)
    w_up2.wait_recv()
    o_far[0].start()
    w_down2.wait_recv()
    o_far[1].start()
    pair_in(2)
    y_in(1)
    pair_in(3)
    y_in(2)
    y_in(3)
    for copy in (o_up, o_down, *o_far):
        copy.wait_recv()
    for copy in (*to_mate, *relay_pair, *relay_up, *relay_down, *g_mate):
        copy.wait_recv()
    mail.finish()
    for copy in locals_[3:]:
        copy.wait()


def view_pass(bias_ref, view, q, g, k_ref, v_ref, kt, vt, gt, st, dp, pb, gs):
    lane = lax.broadcasted_iota(jnp.int32, (1, 128), 1)
    outs, dqs, qms, gms = [], [], [], []
    for h in range(2):
        mine = (lane >= 64) if h else (lane < 64)
        qm = jnp.where(mine, q, jnp.zeros_like(q))
        gm = jnp.where(mine, g, jnp.zeros_like(g))
        qms.append(qm)
        gms.append(gm)
        tops = []
        for j in range(6):
            rows = pl.ds(j * TOK, TOK)
            s = dot(k_ref[pl.ds((2 * view + j) * TOK, TOK), :], qm, NT)
            st[h, rows, :] = s
            tops.append(jnp.max(s, axis=0, keepdims=True) * (SCALE * LOG2E) + bias_ref[view, j])
        top = functools.reduce(jnp.maximum, tops)
        total = jnp.zeros((1, TOK), F32)
        for j in range(6):
            rows = pl.ds(j * TOK, TOK)
            e = jnp.exp2(st[h, rows, :] * (SCALE * LOG2E) - (top - bias_ref[view, j]))
            st[h, rows, :] = e
            total = total + jnp.sum(e, axis=0, keepdims=True)
        inv = 1.0 / total
        for j in range(6):
            rows = pl.ds(j * TOK, TOK)
            p = st[h, rows, :] * inv
            st[h, rows, :] = p
            pb[rows, h * TOK:(h + 1) * TOK] = p.astype(BF)
        ot = dot(vt, pb[:, h * TOK:(h + 1) * TOK])[h * 64:(h + 1) * 64]
        outs.append(ot)
        delta = jnp.sum(gt[h * 64:(h + 1) * 64] * ot, axis=0, keepdims=True)
        for j in range(6):
            rows = pl.ds(j * TOK, TOK)
            d = dot(v_ref[pl.ds((2 * view + j) * TOK, TOK), :], gm, NT)
            gs[rows, h * TOK:(h + 1) * TOK] = (st[h, rows, :] * (d - delta)).astype(BF)
        dqs.append(dot(kt, gs[:, h * TOK:(h + 1) * TOK])[h * 64:(h + 1) * 64])
    return (
        jnp.concatenate(outs, axis=0),
        jnp.concatenate(dqs, axis=0) * SCALE,
        jnp.concatenate(qms, axis=0),
        jnp.concatenate(gms, axis=0),
    )


def attn_kernel(bias_ref, q_ref, g_ref, k_ref, v_ref, att_ref, dq_ref, own_ref, term_ref, st, dp, pb, gs):
    kt = k_ref[0].T
    vt = v_ref[0].T
    k, v = k_ref.at[0], v_ref.at[0]
    held = []
    for view in range(2):
        rows = pl.ds(view * TOK, TOK)
        q, g = q_ref[0, rows, :], g_ref[0, rows, :]
        gt = g.astype(F32).T
        span = slice(2 * view * TOK, (2 * view + 6) * TOK)
        pbv, gsv = pb.at[view], gs.at[view]
        ot, dqt, qm, gm = view_pass(
            bias_ref, view, q, g, k, v, kt[:, span], vt[:, span], gt, st.at[view], dp, pbv, gsv
        )
        att_ref[0, rows, :] = ot.T.astype(BF)
        dq_ref[0, rows, :] = dqt.T.astype(BF)
        held.append((qm, gm))
    for b in range(8):
        parts = []
        for view in range(2):
            j = b - 2 * view
            if 0 <= j < 6:
                qm, gm = held[view]
                rows = pl.ds(j * TOK, TOK)
                dk = dot(gs[view, rows, :], qm) * SCALE
                dv = dot(pb[view, rows, :], gm)
                parts.append((dk, dv))
        dk, dv = parts[0]
        if b in (3, 4):
            own = b - 3
            other = parts[1 - own]
            mine = parts[own]
            rows = pl.ds(own * TOK, TOK)
            own_ref[0, 0, rows, :] = mine[0] + other[0].astype(BF).astype(F32)
            own_ref[1, 0, rows, :] = mine[1] + other[1].astype(BF).astype(F32)
        else:
            if len(parts) == 2:
                dk = dk.astype(BF).astype(F32) + parts[1][0].astype(BF).astype(F32)
                dv = dv.astype(BF).astype(F32) + parts[1][1].astype(BF).astype(F32)
            n, w = {0: (2, 0), 1: (0, 0), 2: (0, 1), 5: (1, 0), 6: (1, 1), 7: (2, 1)}[b]
            rows = pl.ds(w * TOK, TOK)
            term_ref[n, 0, 0, rows, :] = dk.astype(BF)
            term_ref[n, 1, 0, rows, :] = dv.astype(BF)


def attention(bias, q, g, kv):
    S = q.shape[0]
    W = q.shape[2]
    pairs = W // 128
    return pl.pallas_call(
        attn_kernel,
        grid=(pairs, S),
        in_specs=[
            pl.BlockSpec(memory_space=pltpu.SMEM),
            pl.BlockSpec((1, 512, 128), lambda p, s: (s, 0, p)),
            pl.BlockSpec((1, 512, 128), lambda p, s: (s, 0, p)),
            pl.BlockSpec((1, 2048, 128), lambda p, s: (s, 0, p)),
            pl.BlockSpec((1, 2048, 128), lambda p, s: (s, 0, pairs + p)),
        ],
        out_specs=[
            pl.BlockSpec((1, 512, 128), lambda p, s: (s, 0, p)),
            pl.BlockSpec((1, 512, 128), lambda p, s: (s, 0, p)),
            pl.BlockSpec((2, 1, 512, 128), lambda p, s: (0, s, 0, p)),
            pl.BlockSpec((3, 2, 1, 512, 128), lambda p, s: (0, 0, s, 0, p)),
        ],
        out_shape=[
            jax.ShapeDtypeStruct((S, 512, W), BF),
            jax.ShapeDtypeStruct((S, 512, W), BF),
            jax.ShapeDtypeStruct((2, S, 512, W), F32),
            jax.ShapeDtypeStruct((3, 2, S, 512, W), BF),
        ],
        scratch_shapes=[
            pltpu.VMEM((2, 2, 1536, TOK), F32),
            pltpu.VMEM((8, 128), F32),
            pltpu.VMEM((2, 1536, 2 * TOK), BF),
            pltpu.VMEM((2, 1536, 2 * TOK), BF),
        ],
        compiler_params=pltpu.CompilerParams(vmem_limit_bytes=60 * 2**20),
    )(bias, q, g, kv, kv)


def terms_kernel(term_ref, own_ref, dq_ref, att_ref, gp_ref, att_full, inbox, joined, local, send, recv):
    me = Place()
    c = me.core
    mail = Mail(send, recv)
    samples = dq_ref.shape[0]
    width = dq_ref.shape[2]
    parts = [(i, s) for i in range(2) for s in range(samples)]
    greet((me.up, me.down, me.pair, me.mate))
    first, last = me.y == 0, me.y == me.ys - 1
    ups = [mail.copy(term_ref.at[1, i, s], inbox.at[1, i, s], me.up) for i, s in parts]
    downs = [mail.copy(term_ref.at[0, i, s], inbox.at[0, i, s], me.down) for i, s in parts]
    pairs = [mail.copy(term_ref.at[2, i, s], inbox.at[2, i, s], me.pair) for i, s in parts]
    n = len(parts)
    pairs_joined = [mail.again(2 * n + a, joined.at[i, s], inbox.at[2, i, s], me.pair) for a, (i, s) in enumerate(parts)]
    edge = jnp.logical_or(first, last)
    for a in range(n):
        ups[a].start()
        downs[a].start()

        @pl.when(jnp.logical_not(edge))
        def _(a=a):
            pairs[a].start()
    mine = at(c * width, width)
    att_mate = [mail.copy(att_ref.at[s, at((1 - c) * TOK, TOK)], att_full.at[s, :, mine], me.mate) for s in range(samples)]
    for copy in att_mate:
        copy.start()
    att_own = [pltpu.make_async_copy(att_ref.at[s, at(c * TOK, TOK)], att_full.at[s, :, mine], local.at[s]) for s in range(samples)]
    for copy in att_own:
        copy.start()
    gp_ref[:, :, :width] = dq_ref[...]
    for a, (i, s) in enumerate(parts):
        ups[a].wait_recv()
        downs[a].wait_recv()

        @pl.when(first)
        def _(a=a, i=i, s=s):
            joined[i, s] = (term_ref[2, i, s].astype(F32) + inbox[1, i, s].astype(F32)).astype(BF)
            pairs_joined[a].start()

        @pl.when(last)
        def _(a=a, i=i, s=s):
            joined[i, s] = (term_ref[2, i, s].astype(F32) + inbox[0, i, s].astype(F32)).astype(BF)
            pairs_joined[a].start()
    from_down = jnp.where(first, 0.0, 1.0)
    from_up = jnp.where(last, 0.0, 1.0)
    for a, (i, s) in enumerate(parts):
        pairs[a].wait_recv()
        total = own_ref[i, s] + inbox[2, i, s].astype(F32)
        total = total + inbox[1, i, s].astype(F32) * from_down + inbox[0, i, s].astype(F32) * from_up
        gp_ref[s, :, (1 + i) * width:(2 + i) * width] = total.astype(BF)
    for copy in att_mate:
        copy.wait_recv()
    for copy in att_own:
        copy.wait()
    mail.finish()


def reduce_kernel(dw_ref, dl_ref, dw_out, dl_out, *scratch):
    (dl_in, z1u, z1d, z2u, z2d, sent_u, sent_d, zsum, xin, xa_in, xa, q1u, q1d, q2u, q2d, qsent_u, qsent_d,
     whole, v1, vsum, v2, last_own, lastg, mate_in, send, recv) = scratch
    me = Place()
    c = me.core
    mail = Mail(send, recv)
    rows = dw_ref.shape[2]
    width = dw_ref.shape[3]
    hw = width // 2
    qw = width // 4
    greet((me.up, me.down, me.over, me.pair, me.mate, me.z_up, me.z_down, me.outer))
    z, xh = me.z, me.x_hi
    zu, zd, zf = (z + 1) % 4, (z + 3) % 4, (z + 2) % 4
    H1, H2 = pl.ds(0, qw), pl.ds(qw, qw)
    H3, H4 = pl.ds(hw, qw), pl.ds(hw + qw, qw)
    ZC, XC = pl.ds(0, hw), pl.ds(hw, hw)
    a1u = mail.copy(dw_ref.at[:, zf, :, H1], z1u, me.z_up)
    a1d = mail.copy(dw_ref.at[:, zf, :, H2], z1d, me.z_down)
    bx = mail.copy(dw_ref.at[1 - xh, :, :, XC], xa_in, me.outer)
    dlm = mail.copy(dl_ref.at[:, 1 - c], dl_in, me.mate)
    for copy in (a1u, a1d, bx, dlm):
        copy.start()
    sent_u[:, :, qw:] = dw_ref[:, zu, :, qw:hw]
    sent_d[:, :, :qw] = dw_ref[:, zd, :, :qw]
    a1u.wait_recv()
    sent_u[:, :, :qw] = (dw_ref[:, zu, :, :qw].astype(F32) + z1u[...].astype(F32)).astype(BF)
    a2u = mail.copy(sent_u, z2u, me.z_up)
    a2u.start()
    a1d.wait_recv()
    sent_d[:, :, qw:] = (dw_ref[:, zd, :, qw:hw].astype(F32) + z1d[...].astype(F32)).astype(BF)
    a2d = mail.copy(sent_d, z2d, me.z_down)
    a2d.start()
    a2u.wait_recv()
    a2d.wait_recv()
    zsum[...] = (dw_ref[:, z, :, :hw].astype(F32) + z2u[...].astype(F32) + z2d[...].astype(F32)).astype(BF)
    ax = mail.copy(zsum.at[1 - xh], xin, me.outer)
    ax.start()
    bx.wait_recv()
    xa[...] = (dw_ref[xh, :, :, hw:].astype(F32) + xa_in[...].astype(F32)).astype(BF)
    b1u = mail.copy(xa.at[zf, :, pl.ds(0, qw)], q1u, me.z_up)
    b1d = mail.copy(xa.at[zf, :, pl.ds(qw, qw)], q1d, me.z_down)
    b1u.start()
    b1d.start()
    qsent_u[:, qw:] = xa[zu, :, qw:]
    qsent_d[:, :qw] = xa[zd, :, :qw]
    b1u.wait_recv()
    qsent_u[:, :qw] = (xa[zu, :, :qw].astype(F32) + q1u[...].astype(F32)).astype(BF)
    b2u = mail.copy(qsent_u, q2u, me.z_up)
    b2u.start()
    b1d.wait_recv()
    qsent_d[:, qw:] = (xa[zd, :, qw:].astype(F32) + q1d[...].astype(F32)).astype(BF)
    b2d = mail.copy(qsent_d, q2d, me.z_down)
    b2d.start()
    ax.wait_recv()
    whole[:, :hw] = (zsum[xh].astype(F32) + xin[...].astype(F32)).astype(BF)
    dlm.wait_recv()
    dl_out[...] = (dl_ref[:, c].astype(F32) + dl_in[...].astype(F32)).astype(BF)
    b2u.wait_recv()
    b2d.wait_recv()
    whole[:, hw:] = (xa[z, :, :].astype(F32) + q2u[...].astype(F32) + q2d[...].astype(F32)).astype(BF)
    hr, er = rows // 2, rows // 8
    xl, y = me.x_lo, me.y
    p1 = mail.copy(whole.at[at((1 - xl) * hr, hr)], v1, me.pair)
    p1.start()
    p1.wait_recv()
    vsum[...] = (whole[at(xl * hr, hr)].astype(F32) + v1[...].astype(F32)).astype(BF)
    ring = [mail.copy(vsum.at[at(((y + 1 + d) % 4) * er, er)], v2.at[d], to) for d, to in enumerate((me.up, me.over, me.down))]
    for copy in ring:
        copy.start()
    total = vsum[at(y * er, er)].astype(F32)
    for d, copy in enumerate(ring):
        copy.wait_recv()
        total = total + v2[d].astype(F32)
    last_own[...] = total.astype(BF)
    mine = at(xl * hr + y * er, er)
    lastg[mine] = last_own[...]
    back = [mail.copy(last_own, lastg.at[mine], to) for to in (me.up, me.over, me.down)]
    for copy in back:
        copy.start()
    for copy in back:
        copy.wait_recv()
    half = at(xl * hr, hr)
    pb = mail.copy(lastg.at[half], lastg.at[half], me.pair)
    pb.start()
    ma = mail.copy(lastg.at[half], mate_in.at[half], me.mate)
    ma.start()
    pb.wait_recv()
    other = at((1 - xl) * hr, hr)
    mb = mail.copy(lastg.at[other], mate_in.at[other], me.mate)
    mb.start()
    w3 = width // 3
    for k in range(3):
        dw_out[:, pl.ds(pl.multiple_of((2 * k + c) * w3, w3), w3)] = lastg[:, k * w3:(k + 1) * w3].astype(F32)
    ma.wait_recv()
    mb.wait_recv()
    for k in range(3):
        dw_out[:, pl.ds(pl.multiple_of((2 * k + 1 - c) * w3, w3), w3)] = mate_in[:, k * w3:(k + 1) * w3].astype(F32)
    mail.finish()


def pick(values, index):
    return lax.dynamic_index_in_dim(values, index, 0, keepdims=False)


def local(latents, w_qkv, cycle_links, cross_links, d_attended):
    _, _, samples, toks, model = latents.shape
    rows, wide = w_qkv.shape
    half = model // 2
    lat = latents[0, 0]
    view = lax.axis_index("view")
    a = view - view % 2
    ANY = pl.BlockSpec(memory_space=pl.ANY)
    VM = pl.BlockSpec(memory_space=pltpu.VMEM)
    n = 48
    lat_all, w_all, g_all = pl.pallas_call(
        gather_kernel,
        in_specs=[ANY] * 3,
        out_specs=[ANY] * 3,
        out_shape=[
            jax.ShapeDtypeStruct((samples, 8, toks, model), BF),
            jax.ShapeDtypeStruct((model, wide // 2), BF),
            jax.ShapeDtypeStruct((samples, 2 * toks, half), BF),
        ],
        scratch_shapes=[pltpu.SemaphoreType.DMA((7,)), pltpu.SemaphoreType.DMA((n,)), pltpu.SemaphoreType.DMA((n,))],
        compiler_params=pltpu.CompilerParams(collective_id=0, has_side_effects=True, vmem_limit_bytes=VMEM_LIMIT),
    )(lat, w_qkv, d_attended[0, 0])

    cycle, cross = cycle_links[0], cross_links[0]
    one = jnp.ones((), jnp.int32)

    def cyc(at_view):
        return pick(cycle, (at_view + 16) % 16)

    links = jnp.stack([
        jnp.stack([pick(cross, a % 8), cyc(a - 2), one, one, one, cyc(a)]),
        jnp.stack([cyc(a - 1), one, one, one, cyc(a + 1), pick(cross, (a + 1) % 8)]),
    ])
    bias = jnp.where(links > 0, 0.0, -1e30).astype(F32)

    kv = jnp.dot(lat_all.reshape(-1, model), w_all[:, half:], preferred_element_type=F32).astype(BF)
    kv = kv.reshape(samples, 8 * toks, 2 * half)
    lat_own = lat_all[:, 3:5].reshape(-1, model)
    q = jnp.dot(lat_own, w_all[:, :half], preferred_element_type=F32).astype(BF).reshape(samples, 2 * toks, half)
    att, dq, own, terms = attention(bias, q, g_all, kv)

    big = (2, samples, 2 * toks, half)
    gp, att_full = pl.pallas_call(
        terms_kernel,
        in_specs=[VM] * 4,
        out_specs=[VM, ANY],
        out_shape=[
            jax.ShapeDtypeStruct((samples, 2 * toks, 3 * half), BF),
            jax.ShapeDtypeStruct((samples, toks, model), BF),
        ],
        scratch_shapes=[
            pltpu.VMEM((3, *big), BF),
            pltpu.VMEM(big, BF),
            pltpu.SemaphoreType.DMA((2,)),
            pltpu.SemaphoreType.DMA((n,)),
            pltpu.SemaphoreType.DMA((n,)),
        ],
        compiler_params=pltpu.CompilerParams(collective_id=1, has_side_effects=True, vmem_limit_bytes=VMEM_LIMIT),
    )(terms, own, dq, att)

    gp = gp.reshape(-1, 3 * half)
    dl = dot(gp, w_all, NT).reshape(samples, 2, toks, model)
    dw = dot(lat_own, gp, TN).astype(BF).reshape(2, 4, rows, 3 * half)
    w = 3 * half
    h, qt = w // 2, w // 4
    dw_out, dl_out = pl.pallas_call(
        reduce_kernel,
        in_specs=[VM] * 2,
        out_specs=[VM] * 2,
        out_shape=[
            jax.ShapeDtypeStruct((rows, wide), F32),
            jax.ShapeDtypeStruct((samples, toks, model), BF),
        ],
        scratch_shapes=[
            pltpu.VMEM((samples, toks, model), F32),
            *[pltpu.VMEM((2, rows, qt), BF)] * 2,
            *[pltpu.VMEM((2, rows, h), BF)] * 4,
            pltpu.VMEM((2, rows, h), BF),
            pltpu.VMEM((rows, h), BF),
            *[pltpu.VMEM((4, rows, h), BF)] * 2,
            *[pltpu.VMEM((rows, qt), BF)] * 2,
            *[pltpu.VMEM((rows, h), BF)] * 4,
            pltpu.VMEM((rows, w), BF),
            *[pltpu.VMEM((rows // 2, w), BF)] * 2,
            pltpu.VMEM((3, rows // 8, w), BF),
            pltpu.VMEM((rows // 8, w), BF),
            *[pltpu.VMEM((rows, w), BF)] * 2,
            pltpu.SemaphoreType.DMA((n,)),
            pltpu.SemaphoreType.DMA((n,)),
        ],
        compiler_params=pltpu.CompilerParams(collective_id=2, has_side_effects=True, vmem_limit_bytes=VMEM_LIMIT),
    )(dw, dl)
    return att_full[None, None], dl_out[None, None], dw_out


def solution(mesh):
    wide = P("fsdp", "view", None, None, None)
    rows = P("fsdp", None)
    return jax.shard_map(
        local,
        mesh=mesh,
        in_specs=(wide, rows, rows, rows, wide),
        out_specs=(wide, wide, rows),
        check_vma=False,
    )
```

time: 953 us -> 294 us (0.31)
  waiting for transfers between devices: 544 us -> 0 us
  Pallas kernels: 0 us -> 252 us
  local copies, waits for them, and re-layouts: 193 us -> 15.2 us
  matrix products: 125 us -> 24.9 us
  other arithmetic: 38.5 us -> 0.58 us
  starting transfers between devices: 33.8 us -> 0 us
  between operations: 15.1 us -> 0.82 us
    pallas_call x0 -> x4, Pallas kernels: none -> 252 us  [the longest x1 69.3 us: local(): pl.pallas_call(terms_kernel, in_specs=[VM] * 4, out_specs=[VM, ANY], out_...]
    reduce_scatter x1 -> x0, waiting for transfers between devices: 172 us -> none  [local(): lax.psum_scatter(lax.dot_general(flat_rows, grad_proj, (((0,), (0,)), (()...]
    ppermute x10 -> x0, waiting for transfers between devices: 162 us -> none  [passed_along(): lax.ppermute(shard, axis, [(i, (i + by) % peers) for i in range(peers)])]
    psum x1 -> x0, waiting for transfers between devices: 114 us -> none  [local(): grad_weight = lax.psum(partial_rows, 'view')]
    all_gather x1 -> x0, waiting for transfers between devices: 94.3 us -> none  [local(): weights = lax.all_gather(w_qkv, 'fsdp', axis=0, tiled=True)]
    while x169 -> x0, local copies, waits for them, and re-layouts: 77.9 us -> none
    dot_general x43 -> x4, matrix products: 87.5 us -> 24.9 us  [the longest x2 11.9 us: dot(): return lax.dot_general(a, b, dims, preferred_element_type=F32)]
    dynamic_update_slice x56 -> x0, local copies, waits for them, and re-layouts: 42.4 us -> none  [the longest x8 13.4 us: group_step(): lax.dynamic_update_slice_in_dim(own_grads, grad_k[:, :tokens_view], colum...]
  transfers between devices with their start and end apart: 13 -> 0, of which waited for: 9 -> 0; matrix products, arithmetic and copies ran while one was open for 2% -> 0% of each run, Pallas kernels for 0% -> 0%
where the time goes in v1:
time: 294 us
  Pallas kernels  252 us (86%)
  matrix products  24.9 us (8%)
  local copies, waits for them, and re-layouts  15.2 us (5%)
    pallas_call x1, Pallas kernels, local(): pl.pallas_call(terms_kernel, in_specs=[VM] * 4, out_specs=[VM, ANY], out_...  69.3 us
    pallas_call x1, Pallas kernels, local(): pl.pallas_call(gather_kernel, in_specs=[ANY] * 3, out_specs=[ANY] * 3, ou...  61.6 us
    pallas_call x1, Pallas kernels, attention(): pl.pallas_call(attn_kernel, grid=(pairs, S), in_specs=[pl.BlockSpec(memor...  60.9 us
    pallas_call x1, Pallas kernels, local(): pl.pallas_call(reduce_kernel, in_specs=[VM] * 2, out_specs=[VM] * 2, out_...  60.3 us
    dot_general x2, matrix products, dot(): return lax.dot_general(a, b, dims, preferred_element_type=F32)  11.9 us
    dot_general x1, matrix products, local(): jnp.dot(lat_all.reshape(-1, model), w_all[:, half:], preferred_element_ty...  10.8 us
    unnamed x15, local copies, waits for them, and re-layouts  6.53 us

profile of v1, /device:TPU:1, one launch (start us, length us, event | category | flops | bytes accessed | tf_op | source)
XLA Modules:
  0.0 293.7 jit_solution(2423749766622012632)
XLA Ops:
  0.7 1.5 constant_dynamic-slice_fusion.3
  2.2 1.3 constant_dynamic-slice_fusion.5
  3.5 1.9 stack.23
  5.5 2.0 stack.10
  7.5 0.6 compare_select_fusion.bias_ref
  8.0 61.6 %shard_map.76 = (bf16[2,8,256,1024]{3,2,1,0:T(8,128)(2,1)}, bf16[1024,1536]{1,0:T(8,128)(2,1)}, bf16[2,512,512]{2,1,0:T(8,128)(2,1)}) custom-call(bf16[2,256,1024]{2,1,0:T(8,128)(2,1)} %bitcast.37, bf16[128,3072]{1,0:T(8,128)(2,1)} %w_ref.1, bf16[2,256,1024]{2,1,0:T(8,128)(2,1)} %bitcast.38), custom_call_target="tpu_custom_call" | custom-call | tf_op jit(solution)/shard_map/pallas_call | solution.py:511
  69.6 0.0 copy-start.3
  69.6 1.9 slice.9
  71.6 0.6 copy-done.3
  72.1 0.0 copy-start.2
  72.2 2.2 convolution_convert_fusion.2
  74.4 1.5 copy-done.2
  75.9 10.8 %convolution_convert_fusion = bf16[4096,1024]{1,0:T(8,128)(2,1)} fusion(bf16[4096,1024]{1,0:T(8,128)(2,1)S(1)} %bitcast.39, bf16[1024,1536]{1,0:T(8,128)(2,1)S(1)} %copy-done.3), kind=kOutput, calls=%fused_computation | convolution fusion | flops 8594128896 | bytes 18874368 | tf_op jit(solution)/shard_map/dot_general | solution.py:536
  86.7 60.9 %shard_map.77 = (bf16[2,512,512]{2,1,0:T(8,128)(2,1)}, bf16[2,512,512]{2,1,0:T(8,128)(2,1)}, f32[2,2,512,512]{3,2,1,0:T(8,128)}, bf16[3,2,2,512,512]{4,3,2,1,0:T(8,128)(2,1)}) custom-call(f32[2,6]{1,0:T(2,128)} %compare_select_fusion.bias_ref, bf16[2,512,512]{2,1,0:T(8,128)(2,1)} %bitcast.34, bf16[2,512,512]{2,1,0:T(8,128)(2,1)} %get-tuple-element.16.g_ref, ...), custom_call_target="tpu_custom_call" | custom-call | tf_op jit(solution)/shard_map/pallas_call | solution.py:308
  147.7 69.3 %shard_map.78 = (bf16[2,512,1536]{2,1,0:T(8,128)(2,1)}, bf16[2,256,1024]{2,1,0:T(8,128)(2,1)}) custom-call(bf16[3,2,2,512,512]{4,3,2,1,0:T(8,128)(2,1)} %get-tuple-element.17.term_ref, f32[2,2,512,512]{3,2,1,0:T(8,128)} %get-tuple-element.18.own_ref, bf16[2,512,512]{2,1,0:T(8,128)(2,1)} %get-tuple-element.19.dq_ref, ...), custom_call_target="tpu_custom_call" | custom-call | tf_op jit(solution)/shard_map/pallas_call | solution.py:543
  217.0 0.0 copy-start.4
  217.0 0.0 copy-start.5
  217.0 6.9 %convolution_convert_fusion.1 = bf16[1024,1536]{1,0:T(8,128)(2,1)} fusion(bf16[1024,1024]{1,0:T(8,128)(2,1)S(1)} %bitcast.33, bf16[1024,1536]{1,0:T(8,128)(2,1)} %bitcast.42), kind=kOutput, calls=%fused_computation.1 | convolution fusion | flops 3222798336 | bytes 8388608 | tf_op jit(solution)/shard_map/dot_general | solution.py:83
  223.9 0.0 copy-done.4
  223.9 0.0 copy-done.5
  223.9 5.0 %fusion.dl_ref = f32[2,2,256,1024]{3,2,1,0:T(8,128)} fusion(bf16[2,2,256,1536]{3,2,1,0:T(8,128)(2,1)S(1)} %bitcast.43, bf16[1024,1536]{1,0:T(8,128)(2,1)S(1)} %copy-done.4), kind=kOutput, calls=%fused_computation.2 | convolution fusion | flops 3221225472 | bytes 10485760 | tf_op jit(solution)/shard_map/dot_general | solution.py:83
  228.9 0.0 copy-start.1
  228.9 60.3 %shard_map.79 = (f32[128,3072]{1,0:T(8,128)}, bf16[2,256,1024]{2,1,0:T(8,128)(2,1)}) custom-call(bf16[2,4,128,1536]{3,2,1,0:T(8,128)(2,1)} %bitcast.31, f32[2,2,256,1024]{3,2,1,0:T(8,128)} %fusion.dl_ref), custom_call_target="tpu_custom_call" | custom-call | tf_op jit(solution)/shard_map/pallas_call | solution.py:566
  289.3 0.0 copy-start
  289.3 0.0 copy-done.1
  289.3 1.0 copy.12
  290.3 2.3 copy.13
  292.5 0.0 copy-done
  292.5 1.1 copy.14
  (1 shorter events, 0.0 us)
Async XLA Ops:
  69.6 2.5 copy-start.3
  72.1 3.8 %copy-start.2 = (bf16[2,8,256,1024]{3,2,1,0:T(8,128)(2,1)S(1)}, bf16[2,8,256,1024]{3,2,1,0:T(8,128)(2,1)}, u32[]{:S(2)}) copy-start(bf16[2,8,256,1024]{3,2,1,0:T(8,128)(2,1)} %get-tuple-element.14) | copy-start | bytes 25165828
  217.0 6.9 %copy-start.4 = (bf16[1024,1536]{1,0:T(8,128)(2,1)S(1)}, bf16[1024,1536]{1,0:T(8,128)(2,1)}, u32[]{:S(2)}) copy-start(bf16[1024,1536]{1,0:T(8,128)(2,1)} %get-tuple-element.15) | copy-start | bytes 9437188
  217.0 6.9 %copy-start.5 = (bf16[2,512,1536]{2,1,0:T(8,128)(2,1)S(1)}, bf16[2,512,1536]{2,1,0:T(8,128)(2,1)}, u32[]{:S(2)}) copy-start(bf16[2,512,1536]{2,1,0:T(8,128)(2,1)} %get-tuple-element.22) | copy-start | bytes 9437188
  228.9 60.4 %copy-start.1 = (bf16[2,256,1024]{2,1,0:T(8,128)(2,1)S(1)}, bf16[2,256,1024]{2,1,0:T(8,128)(2,1)}, u32[]{:S(2)}) copy-start(bf16[2,256,1024]{2,1,0:T(8,128)(2,1)} %get-tuple-element.21) | copy-start | bytes 3145732
  289.3 3.3 %copy-start = (f32[128,3072]{1,0:T(8,128)S(1)}, f32[128,3072]{1,0:T(8,128)}, u32[]{:S(2)}) copy-start(f32[128,3072]{1,0:T(8,128)} %get-tuple-element.36) | copy-start | bytes 4718596

commit v2 on v0

v2 whole, which is shorter than its diff:
```python
import functools

import jax
import jax.numpy as jnp
from jax import lax
from jax.experimental import pallas as pl
from jax.experimental.pallas import tpu as pltpu
from jax.sharding import PartitionSpec as P

BF, F32 = jnp.bfloat16, jnp.float32
MESH = pl.DeviceIdType.MESH
TOK = 256
LOG2E = 1.4426950408889634
SCALE = 0.125
NT = (((1,), (1,)), ((), ()))
NN = (((1,), (0,)), ((), ()))
TN = (((0,), (0,)), ((), ()))
VMEM_LIMIT = 60 * 2**20


class Place:
    def __init__(self):
        v, f = lax.axis_index("view"), lax.axis_index("fsdp")
        self.view, self.fsdp = v, f
        self.ys, self.zs = 4, 4
        self.core = v % 2
        self.y = (v // 2) % 4
        self.x_lo = v // 8
        self.z = f % 4
        self.x_hi = f // 4
        column = self.x_lo * 8 + self.core

        def at(view, fsdp):
            return {"view": view, "fsdp": fsdp}

        self.up = at(column + 2 * ((self.y + 1) % 4), f)
        self.down = at(column + 2 * ((self.y + 3) % 4), f)
        self.over = at(column + 2 * ((self.y + 2) % 4), f)
        self.pair = at((v + 8) % 16, f)
        self.mate = at(v + 1 - 2 * self.core, f)
        self.f_up = self.x_hi * 4 + (self.z + 1) % 4
        self.f_down = self.x_hi * 4 + (self.z + 3) % 4
        self.f_far = self.x_hi * 4 + (self.z + 2) % 4
        self.f_outer = (f + 4) % 8
        self.z_up = at(v, self.f_up)
        self.z_down = at(v, self.f_down)
        self.outer = at((v + 8) % 16, self.f_outer)


def greet(devices):
    barrier = pltpu.get_barrier_semaphore()
    for device in devices:
        pl.semaphore_signal(barrier, inc=1, device_id=device, device_id_type=MESH)
    pl.semaphore_wait(barrier, len(devices))


class Mail:
    def __init__(self, send, recv):
        self.send, self.recv, self.made, self.sent = send, recv, 0, []

    def copy(self, src, dst, to):
        i = self.made
        self.made += 1
        made = self.again(i, src, dst, to)
        self.sent.append(made)
        return made

    def again(self, i, src, dst, to):
        return pltpu.make_async_remote_copy(
            src_ref=src, dst_ref=dst, send_sem=self.send.at[i], recv_sem=self.recv.at[i],
            device_id=to, device_id_type=MESH)

    def finish(self):
        for copy in self.sent:
            copy.wait_send()


def at(start, size):
    return pl.ds(pl.multiple_of(start, size), size)


def dot(a, b, dims=NN):
    return lax.dot_general(a, b, dims, preferred_element_type=F32)

def gather_kernel(lat_ref, w_ref, g_ref, lat_all, w_all, g_all, local, send, recv):
    me = Place()
    c = me.core
    rows = w_ref.shape[0]
    half = w_ref.shape[1] // 6
    pairs = half // 128
    samples, toks = lat_ref.shape[0], lat_ref.shape[1]
    chunks = [(s, pl.ds(t * (toks // 4), toks // 4)) for s in range(samples) for t in range(4)]
    own_block, other_block = 3 + c, 4 - c
    strips = []
    for p in range(pairs):
        for k in range(3):
            strips.append(pltpu.make_async_copy(
                w_ref.at[:, at((2 * k + c) * half + p * 128, 128)],
                w_all.at[at(me.fsdp * rows, rows), pl.ds((3 * p + k) * 128, 128)],
                local.at[3 * p + k]))
    kept = []
    base = 3 * pairs
    for s in range(samples):
        kept.append(pltpu.make_async_copy(lat_ref.at[s], lat_all.at[s, own_block], local.at[base + s]))
        kept.append(pltpu.make_async_copy(
            g_ref.at[s, :, at(c * half, half)], g_all.at[s, at(c * toks, toks), :], local.at[base + 2 + s]))
    for copy in strips + kept:
        copy.start()
    greet((me.up, me.down, me.pair, me.mate, me.z_up, me.z_down, me.outer))
    mail = Mail(send, recv)
    remote = mail.copy

    def block(b, chunk):
        s, t = chunk
        return lat_all.at[s, b, t]

    def shard(f, part=None):
        if part is None:
            return w_all.at[at(f * rows, rows)]
        return w_all.at[at(f * rows + part * (rows // 2), rows // 2)]

    n = range(len(chunks))
    mine = [lat_ref.at[s, t] for s, t in chunks]
    up = [remote(mine[i], block(1 + c, chunks[i]), me.up) for i in n]
    down = [remote(mine[i], block(5 + c, chunks[i]), me.down) for i in n]
    up_far = [mail.again(i, block(7 * c, chunks[i]), block(1 + c, chunks[i]), me.up) for i in n]
    down_far = [mail.again(len(chunks) + i, block(7 * c, chunks[i]), block(5 + c, chunks[i]), me.down) for i in n]
    to_pair = [remote(mine[i], block(7 * c, chunks[i]), me.pair) for i in n]
    to_mate = [remote(lat_ref.at[s], lat_all.at[s, own_block], me.mate) for s in range(samples)]
    relays = {b: [remote(lat_all.at[s, bb], lat_all.at[s, bb], me.mate) for s in range(samples)]
              for b, bb in (("pair", 7 * c), ("up", 1 + c), ("down", 5 + c))}
    g_mate = [remote(
        g_ref.at[s, :, at((1 - c) * half, half)], g_all.at[s, at(c * toks, toks), :], me.mate) for s in range(samples)]
    first, last = me.y == 0, me.y == me.ys - 1
    f0, f_up, f_down, f_out, far = me.fsdp, me.f_up, me.f_down, me.f_outer, me.f_far
    w_up = remote(shard(f0), shard(f0), me.z_up)
    w_down = remote(shard(f0), shard(f0), me.z_down)
    w_out = remote(shard(f0), shard(f0), me.outer)
    w_up2 = remote(shard(f_down, 0), shard(f_down, 0), me.z_up)
    w_down2 = remote(shard(f_up, 1), shard(f_up, 1), me.z_down)
    o_up = remote(shard(f_out), shard(f_out), me.z_up)
    o_down = remote(shard(f_out), shard(f_out), me.z_down)
    o_far = [remote(shard(far, part), shard(far, part), me.outer) for part in range(2)]

    to_pair[0].start()
    to_pair[1].start()
    for copy in strips:
        copy.wait()
    w_up.start()
    w_down.start()
    w_out.start()
    for i in n:
        pl.when(jnp.logical_not(last))(up[i].start)
        pl.when(jnp.logical_not(first))(down[i].start)
    for copy in to_mate + g_mate:
        copy.start()
    for i in n:
        to_pair[i].wait_send()
        if i + 2 < len(chunks):
            to_pair[i + 2].start()
        to_pair[i].wait_recv()
        pl.when(last)(up_far[i].start)
        pl.when(first)(down_far[i].start)
        if i == len(chunks) // 2 - 1:
            relays["pair"][0].start()
        if i == 2:
            w_up.wait_recv()
            w_up2.start()
            w_down.wait_recv()
            w_down2.start()
            w_out.wait_recv()
            o_up.start()
            o_down.start()
        if i == 5:
            w_up2.wait_recv()
            o_far[0].start()
            w_down2.wait_recv()
            o_far[1].start()
    relays["pair"][1].start()
    each = len(chunks) // samples
    for s in range(samples):
        for i in range(s * each, (s + 1) * each):
            up[i].wait_recv()
        relays["up"][s].start()
        for i in range(s * each, (s + 1) * each):
            down[i].wait_recv()
        relays["down"][s].start()
    for copy in (o_up, o_down, *o_far, *to_mate, *g_mate, *relays["pair"], *relays["up"], *relays["down"]):
        copy.wait_recv()
    for i, copy in enumerate(mail.sent):
        if not 2 * len(chunks) <= i < 3 * len(chunks):
            copy.wait_send()
    for copy in kept:
        copy.wait()


def when(condition):
    if isinstance(condition, bool):
        return (lambda f: f()) if condition else (lambda f: None)
    return pl.when(condition)


def both(*conditions):
    if any(isinstance(x, bool) and not x for x in conditions):
        return False
    conditions = [x for x in conditions if not isinstance(x, bool)]
    return functools.reduce(jnp.logical_and, conditions) if conditions else True


def view_pass(bias, q, g, k_rows, v_rows, kt, vt, gt, st, pb, gs):
    lane = lax.broadcasted_iota(jnp.int32, (1, 128), 1)
    outs, dqs, qms, gms = [], [], [], []
    for h in range(2):
        mine = (lane >= 64) if h else (lane < 64)
        qm = jnp.where(mine, q, jnp.zeros_like(q))
        gm = jnp.where(mine, g, jnp.zeros_like(g))
        qms.append(qm)
        gms.append(gm)
        tops = []
        for j in range(6):
            rows = pl.ds(j * TOK, TOK)
            s = dot(k_rows(j), qm, NT)
            st[h, rows, :] = s
            tops.append(jnp.max(s, axis=0, keepdims=True) * (SCALE * LOG2E) + bias[j])
        top = functools.reduce(jnp.maximum, tops)
        total = jnp.zeros((1, TOK), F32)
        for j in range(6):
            rows = pl.ds(j * TOK, TOK)
            e = jnp.exp2(st[h, rows, :] * (SCALE * LOG2E) - (top - bias[j]))
            st[h, rows, :] = e
            total = total + jnp.sum(e, axis=0, keepdims=True)
        inv = 1.0 / total
        for j in range(6):
            rows = pl.ds(j * TOK, TOK)
            p = st[h, rows, :] * inv
            st[h, rows, :] = p
            pb[rows, h * TOK:(h + 1) * TOK] = p.astype(BF)
        ot = dot(vt, pb[:, h * TOK:(h + 1) * TOK])[h * 64:(h + 1) * 64]
        outs.append(ot)
        delta = jnp.sum(gt[h * 64:(h + 1) * 64] * ot, axis=0, keepdims=True)
        for j in range(6):
            rows = pl.ds(j * TOK, TOK)
            d = dot(v_rows(j), gm, NT)
            gs[rows, h * TOK:(h + 1) * TOK] = (st[h, rows, :] * (d - delta)).astype(BF)
        dqs.append(dot(kt, gs[:, h * TOK:(h + 1) * TOK])[h * 64:(h + 1) * 64])
    return (
        jnp.concatenate(outs, axis=0),
        jnp.concatenate(dqs, axis=0) * SCALE,
        jnp.concatenate(qms, axis=0),
        jnp.concatenate(gms, axis=0),
    )


def project(lat, w, s, p, k_s, v_s, q_s):
    span = 2 * lat.shape[1] // 8
    first = 3 * span // 2
    w_kv = w[:, at(p * 384 + 128, 128)], w[:, at(p * 384 + 256, 128)]
    w_kv = jnp.concatenate(w_kv, axis=1)
    for r in range(lat.shape[1] // span):
        rows = pl.ds(r * span, span)
        kv = dot(lat[s, rows, :], w_kv).astype(BF)
        k_s[rows, :] = kv[:, :128]
        v_s[rows, :] = kv[:, 128:]
    q_s[...] = dot(lat[s, pl.ds(first, span), :], w[:, at(p * 384, 128)]).astype(BF)


def attend(bias, s, p, g_ref, k_s, v_s, q_s, st, pb, gs, att, dq, own, term):
    kt = k_s[...].T
    vt = v_s[...].T
    held = []
    for view in range(2):
        rows = pl.ds(view * TOK, TOK)
        q = q_s[rows, :]
        g = g_ref[s, rows, at(p * 128, 128)]
        gt = g.astype(F32).T
        span = slice(2 * view * TOK, (2 * view + 6) * TOK)

        def rows_of(ref, view=view):
            return lambda j: ref[pl.ds((2 * view + j) * TOK, TOK), :]

        ot, dqt, qm, gm = view_pass(
            bias[view], q, g, rows_of(k_s), rows_of(v_s), kt[:, span], vt[:, span], gt,
            st.at[view], pb.at[view], gs.at[view])
        att[rows, :] = ot.T.astype(BF)
        dq[rows, :] = dqt.T.astype(BF)
        held.append((qm, gm))
    for b in range(8):
        parts = []
        for view in range(2):
            j = b - 2 * view
            if 0 <= j < 6:
                qm, gm = held[view]
                rows = pl.ds(j * TOK, TOK)
                dk = dot(gs[view, rows, :], qm) * SCALE
                dv = dot(pb[view, rows, :], gm)
                parts.append((dk, dv))
        dk, dv = parts[0]
        if b in (3, 4):
            w = b - 3
            mine, other = parts[w], parts[1 - w]
            rows = pl.ds(w * TOK, TOK)
            own[0, rows, :] = mine[0] + other[0].astype(BF).astype(F32)
            own[1, rows, :] = mine[1] + other[1].astype(BF).astype(F32)
        else:
            if len(parts) == 2:
                dk = dk.astype(BF).astype(F32) + parts[1][0].astype(BF).astype(F32)
                dv = dv.astype(BF).astype(F32) + parts[1][1].astype(BF).astype(F32)
            n, w = {0: (2, 0), 1: (0, 0), 2: (0, 1), 5: (1, 0), 6: (1, 1), 7: (2, 1)}[b]
            rows = pl.ds(w * TOK, TOK)
            term[n, 0, rows, :] = dk.astype(BF)
            term[n, 1, rows, :] = dv.astype(BF)


STEPS = 8
KINDS = ("a1u", "a1d", "bx", "a2u", "a2d", "b1u", "b1d", "ax", "b2u", "b2d", "p1", "r0", "r1", "r2", "g0", "g1", "g2", "pb", "ma", "mb")


def main_kernel(cycle_ref, cross_ref, lat_hbm, w_hbm, g_hbm, att_full, dw_out, dl_out,
                lat, w, g, k_s, v_s, q_s, st, pb, gs, att, own, out, inbox, gp, dwb, dl_out_s, dl_in,
                z1u, z1d, z2u, z2d, su, sd, zs, xin, xain, xa, q1u, q1d, q2u, q2d, qsu, qsd,
                whole, v1, vsum, v2, fin, fing, mate_in,
                local, tsend, trecv, rsend, rrecv, dsend, drecv):
    me = Place()
    c, y, z, xh, xl = me.core, me.y, me.z, me.x_hi, me.x_lo
    zu, zd, zf = (z + 1) % 4, (z + 3) % 4, (z + 2) % 4
    width = 512
    loads = [pltpu.make_async_copy(w_hbm, w, local.at[0]), pltpu.make_async_copy(lat_hbm.at[0], lat.at[0], local.at[1]),
             pltpu.make_async_copy(g_hbm, g, local.at[2]), pltpu.make_async_copy(lat_hbm.at[1], lat.at[1], local.at[3])]
    for copy in loads:
        copy.start()
    greet((me.up, me.down, me.over, me.pair, me.mate, me.z_up, me.z_down, me.outer))

    def weight(link):
        return jnp.where(link > 0, 0.0, -1e30).astype(F32)

    a = me.view - c

    def cyc(v):
        return weight(cycle_ref[(v + 16) % 16])

    bias = [
        [weight(cross_ref[a % 8]), cyc(a - 2), 0.0, 0.0, 0.0, cyc(a)],
        [cyc(a - 1), 0.0, 0.0, 0.0, cyc(a + 1), weight(cross_ref[(a + 1) % 8])],
    ]
    first, last = y == 0, y == 3
    edge = jnp.logical_or(first, last)
    keep_down = jnp.where(first, 0.0, 1.0)
    keep_up = jnp.where(last, 0.0, 1.0)

    def mail(src, dst, send, recv, to):
        return pltpu.make_async_remote_copy(
            src_ref=src, dst_ref=dst, send_sem=send, recv_sem=recv, device_id=to, device_id_type=MESH)

    def up(t):
        return mail(out.at[t % 3, 1], inbox.at[t, 1], tsend.at[0, t % 3], trecv.at[0, t], me.up)

    def down(t):
        return mail(out.at[t % 3, 0], inbox.at[t, 0], tsend.at[1, t % 3], trecv.at[1, t], me.down)

    def across(t):
        return mail(out.at[t % 3, 2], inbox.at[t, 2], tsend.at[2, t % 3], trecv.at[2, t], me.pair)

    def columns(t):
        return at(c * width + (t // 2) * 128, 128)

    def att_mate(t):
        return mail(att.at[t % 3, at((1 - c) * TOK, TOK)], att_full.at[t % 2, :, columns(t)],
                    tsend.at[3, t % 3], trecv.at[3, t], me.mate)

    def att_own(t):
        return pltpu.make_async_copy(
            att.at[t % 3, at(c * TOK, TOK)], att_full.at[t % 2, :, columns(t)], tsend.at[4, t % 3])

    def red(kind, p, src, dst, to):
        i = KINDS.index(kind)
        return mail(src, dst, rsend.at[i, p], rrecv.at[i, p], to)

    lo, hi, top, low = pl.ds(0, 32), pl.ds(32, 32), pl.ds(0, 64), pl.ds(64, 64)
    hr, er = 64, 16
    mine = at(xl * hr + y * er, er)
    half = at(xl * hr, hr)
    other = at((1 - xl) * hr, hr)

    def a1u(p):
        return red("a1u", p, dwb.at[p, :, zf, lo], z1u.at[p], me.z_up)

    def a1d(p):
        return red("a1d", p, dwb.at[p, :, zf, hi], z1d.at[p], me.z_down)

    def bx(p):
        return red("bx", p, dwb.at[p, 1 - xh, :, low], xain.at[p], me.outer)

    def a2u(p):
        return red("a2u", p, su.at[p], z2u.at[p], me.z_up)

    def a2d(p):
        return red("a2d", p, sd.at[p], z2d.at[p], me.z_down)

    def b1u(p):
        return red("b1u", p, xa.at[p, zf, lo], q1u.at[p], me.z_up)

    def b1d(p):
        return red("b1d", p, xa.at[p, zf, hi], q1d.at[p], me.z_down)

    def ax(p):
        return red("ax", p, zs.at[p, 1 - xh], xin.at[p], me.outer)

    def b2u(p):
        return red("b2u", p, qsu.at[p], q2u.at[p], me.z_up)

    def b2d(p):
        return red("b2d", p, qsd.at[p], q2d.at[p], me.z_down)

    def p1(p):
        return red("p1", p, whole.at[p, other], v1.at[p], me.pair)

    def ring(p):
        return [red(f"r{d}", p, vsum.at[p, at(((y + 1 + d) % 4) * er, er)], v2.at[p, d], to)
                for d, to in enumerate((me.up, me.over, me.down))]

    def back(p):
        return [red(f"g{d}", p, fin.at[p], fing.at[p, mine], to) for d, to in enumerate((me.up, me.over, me.down))]

    def pair_back(p):
        return red("pb", p, fing.at[p, half], fing.at[p, half], me.pair)

    def mate_half(p):
        return red("ma", p, fing.at[p, half], mate_in.at[p, half], me.mate)

    def mate_other(p):
        return red("mb", p, fing.at[p, other], mate_in.at[p, other], me.mate)

    def f32(x):
        return x.astype(F32)

    def weight_grad(p):
        for f in range(8):
            total = None
            for s in range(2):
                part = dot(lat[s, pl.ds(3 * TOK, 2 * TOK), f * 128:(f + 1) * 128], gp[p, pl.ds(s * 512, 512), :], TN)
                total = part if total is None else total + part
            dwb[p, f // 4, f % 4] = total.astype(BF)

    def phase1(p):
        weight_grad(p)
        for make in (a1u, a1d, bx):
            make(p).start()

    def phase2(p):
        a1u(p).wait_recv()
        a1d(p).wait_recv()
        su[p, :, lo] = (f32(dwb[p, :, zu, lo]) + f32(z1u[p])).astype(BF)
        su[p, :, hi] = dwb[p, :, zu, hi]
        sd[p, :, lo] = dwb[p, :, zd, lo]
        sd[p, :, hi] = (f32(dwb[p, :, zd, hi]) + f32(z1d[p])).astype(BF)
        a2u(p).start()
        a2d(p).start()
        bx(p).wait_recv()
        xa[p] = (f32(dwb[p, xh, :, low]) + f32(xain[p])).astype(BF)
        b1u(p).start()
        b1d(p).start()

    def phase3(p):
        b1u(p).wait_recv()
        b1d(p).wait_recv()
        qsu[p, lo] = (f32(xa[p, zu, lo]) + f32(q1u[p])).astype(BF)
        qsu[p, hi] = xa[p, zu, hi]
        qsd[p, lo] = xa[p, zd, lo]
        qsd[p, hi] = (f32(xa[p, zd, hi]) + f32(q1d[p])).astype(BF)
        b2u(p).start()
        b2d(p).start()
        a2u(p).wait_recv()
        a2d(p).wait_recv()
        zs[p] = (f32(dwb[p, :, z, top]) + f32(z2u[p]) + f32(z2d[p])).astype(BF)
        ax(p).start()

    def phase4(p):
        b2u(p).wait_recv()
        b2d(p).wait_recv()
        whole[p, low] = (f32(xa[p, z]) + f32(q2u[p]) + f32(q2d[p])).astype(BF)
        ax(p).wait_recv()
        whole[p, top] = (f32(zs[p, xh]) + f32(xin[p])).astype(BF)
        p1(p).start()

    def phase5(p):
        p1(p).wait_recv()
        vsum[p] = (f32(whole[p, half]) + f32(v1[p])).astype(BF)
        for copy in ring(p):
            copy.start()

    def phase6(p):
        total = f32(vsum[p, at(y * er, er)])
        for d, copy in enumerate(ring(p)):
            copy.wait_recv()
            total = total + f32(v2[p, d])
        fin[p] = total.astype(BF)
        fing[p, mine] = total.astype(BF)
        for copy in back(p):
            copy.start()

    def phase7(p):
        for copy in back(p):
            copy.wait_recv()
        pair_back(p).start()
        mate_half(p).start()

    def phase8(p):
        pair_back(p).wait_recv()
        mate_other(p).start()

    phases = (phase1, phase2, phase3, phase4, phase5, phase6, phase7, phase8)

    def gather_grads(t):
        across(t).wait_recv()
        s, p = t % 2, t // 2
        for i in range(2):
            total = own[t % 3, i] + f32(inbox[t, 2, i]) + f32(inbox[t, 1, i]) * keep_down + f32(inbox[t, 0, i]) * keep_up
            gp[p, at(s * 512, 512), (1 + i) * 128:(2 + i) * 128] = total.astype(BF)

    def service(t):
        @when(both(t >= 1, t <= STEPS))
        def _():
            u = t - 1
            up(u).wait_recv()
            down(u).wait_recv()

            @pl.when(first)
            def _():
                out[u % 3, 2] = (f32(out[u % 3, 2]) + f32(inbox[u, 1])).astype(BF)

            @pl.when(last)
            def _():
                out[u % 3, 2] = (f32(out[u % 3, 2]) + f32(inbox[u, 0])).astype(BF)

            @pl.when(edge)
            def _():
                across(u).start()

        when(both(t >= 2, t <= STEPS + 1))(lambda: gather_grads(t - 2))
        for k, phase in enumerate(phases):
            if isinstance(t, int) or k < 5:
                due = t - 3 - k
                when(both(due >= 0, due <= 6, due % 2 == 0))(lambda: phase(due // 2))

    loads[0].wait()
    loads[1].wait()
    loads[2].wait()

    def step(t, carry):
        s, p = t % 2, t // 2

        @pl.when(t == 1)
        def _():
            loads[3].wait()

        @pl.when(t >= 3)
        def _():
            u = t - 3
            up(u).wait_send()
            down(u).wait_send()
            across(u).wait_send()
            att_mate(u).wait_send()
            att_own(u).wait()

        project(lat, w, s, p, k_s, v_s, q_s)
        attend(bias, s, p, g, k_s, v_s, q_s, st, pb, gs, att.at[t % 3], gp.at[p, at(s * 512, 512), pl.ds(0, 128)],
               own.at[t % 3], out.at[t % 3])
        up(t).start()
        down(t).start()

        @pl.when(jnp.logical_not(edge))
        def _():
            across(t).start()

        att_mate(t).start()
        att_own(t).start()
        service(t)
        return carry

    lax.fori_loop(0, STEPS, step, 0)

    def latent_grad():
        for n in range(4):
            w_n = w[pl.ds(n * 256, 256), :]
            for r in range(4):
                rows = pl.ds(r * 256, 256)
                total = None
                for p in range(4):
                    part = dot(gp[p, rows, :], w_n[:, p * 384:(p + 1) * 384], NT)
                    total = part if total is None else total + part
                st[n // 2, n % 2, rows, :] = total

    def dl_mate():
        return mail(dl_out_s, dl_in, dsend.at[0], drecv.at[0], me.mate)

    service(STEPS)
    service(STEPS + 1)
    latent_grad()
    for s in range(2):
        for n in range(4):
            dl_out_s[s, :, n * 256:(n + 1) * 256] = st[n // 2, n % 2, at(s * 512 + (1 - c) * TOK, TOK), :].astype(BF)
    dl_mate().start()
    service(STEPS + 2)
    service(STEPS + 3)
    dl_mate().wait_recv()
    for s in range(2):
        for n in range(4):
            cols = slice(n * 256, (n + 1) * 256)
            dl_out[s, :, cols] = (st[n // 2, n % 2, at(s * 512 + c * TOK, TOK), :] + f32(dl_in[s, :, cols])).astype(BF)
    for t in range(STEPS + 4, STEPS + 9):
        service(t)
    for p in range(4):
        for k in range(3):
            dw_out[:, at((2 * k + c) * width + p * 128, 128)] = f32(fing[p, :, k * 128:(k + 1) * 128])
        mate_half(p).wait_recv()
        mate_other(p).wait_recv()
        for k in range(3):
            dw_out[:, at((2 * k + 1 - c) * width + p * 128, 128)] = f32(mate_in[p, :, k * 128:(k + 1) * 128])
    for t in range(STEPS - 3, STEPS):
        for make in (up, down, across, att_mate):
            make(t).wait_send()
        att_own(t).wait()
    for t in range(STEPS):
        att_mate(t).wait_recv()
    dl_mate().wait_send()
    for p in range(4):
        for make in (a1u, a1d, bx, a2u, a2d, b1u, b1d, ax, b2u, b2d, p1, pair_back, mate_half, mate_other):
            make(p).wait_send()
        for copy in ring(p) + back(p):
            copy.wait_send()


def local(latents, w_qkv, cycle_links, cross_links, d_attended):
    _, _, samples, toks, model = latents.shape
    rows, wide = w_qkv.shape
    half = model // 2
    ANY = pl.BlockSpec(memory_space=pl.ANY)
    VM = pl.BlockSpec(memory_space=pltpu.VMEM)
    SM = pl.BlockSpec(memory_space=pltpu.SMEM)
    n = 48
    lat_all, w_all, g_all = pl.pallas_call(
        gather_kernel,
        in_specs=[ANY] * 3,
        out_specs=[ANY] * 3,
        out_shape=[
            jax.ShapeDtypeStruct((samples, 8, toks, model), BF),
            jax.ShapeDtypeStruct((model, wide // 2), BF),
            jax.ShapeDtypeStruct((samples, 2 * toks, half), BF),
        ],
        scratch_shapes=[pltpu.SemaphoreType.DMA((16,)), pltpu.SemaphoreType.DMA((n,)), pltpu.SemaphoreType.DMA((n,))],
        compiler_params=pltpu.CompilerParams(collective_id=0, has_side_effects=True, vmem_limit_bytes=VMEM_LIMIT),
    )(latents[0, 0], w_qkv, d_attended[0, 0])

    def vm(*shape, dtype=BF):
        return pltpu.VMEM(shape, dtype)

    W = 384
    att_full, dw_out, dl_out = pl.pallas_call(
        main_kernel,
        in_specs=[SM, SM, ANY, ANY, ANY],
        out_specs=[ANY, VM, VM],
        out_shape=[
            jax.ShapeDtypeStruct((samples, toks, model), BF),
            jax.ShapeDtypeStruct((rows, wide), F32),
            jax.ShapeDtypeStruct((samples, toks, model), BF),
        ],
        scratch_shapes=[
            vm(samples, 8 * toks, model), vm(model, wide // 2), vm(samples, 2 * toks, half),
            vm(8 * toks, 128), vm(8 * toks, 128), vm(2 * toks, 128),
            vm(2, 2, 6 * toks, toks, dtype=F32), vm(2, 6 * toks, 2 * toks), vm(2, 6 * toks, 2 * toks),
            vm(3, 2 * toks, 128), vm(3, 2, 2 * toks, 128, dtype=F32),
            vm(3, 3, 2, 2 * toks, 128), vm(STEPS, 3, 2, 2 * toks, 128),
            vm(4, samples * 2 * toks, W), vm(4, 2, 4, rows, W),
            vm(samples, toks, model), vm(samples, toks, model),
            vm(4, 2, 32, W), vm(4, 2, 32, W),
            vm(4, 2, 64, W), vm(4, 2, 64, W), vm(4, 2, 64, W), vm(4, 2, 64, W), vm(4, 2, 64, W),
            vm(4, 64, W), vm(4, 4, 64, W), vm(4, 4, 64, W),
            vm(4, 32, W), vm(4, 32, W),
            vm(4, 64, W), vm(4, 64, W), vm(4, 64, W), vm(4, 64, W),
            vm(4, rows, W), vm(4, 64, W), vm(4, 64, W), vm(4, 3, 16, W), vm(4, 16, W), vm(4, rows, W), vm(4, rows, W),
            pltpu.SemaphoreType.DMA((4,)),
            pltpu.SemaphoreType.DMA((5, 3)), pltpu.SemaphoreType.DMA((4, STEPS)),
            pltpu.SemaphoreType.DMA((len(KINDS), 4)), pltpu.SemaphoreType.DMA((len(KINDS), 4)),
            pltpu.SemaphoreType.DMA((1,)), pltpu.SemaphoreType.DMA((1,)),
        ],
        compiler_params=pltpu.CompilerParams(collective_id=1, has_side_effects=True, vmem_limit_bytes=63 * 2**20),
    )(cycle_links[0], cross_links[0], lat_all.reshape(samples, 8 * toks, model), w_all, g_all)
    return att_full[None, None], dl_out[None, None], dw_out


def solution(mesh):
    wide = P("fsdp", "view", None, None, None)
    rows = P("fsdp", None)
    return jax.shard_map(
        local,
        mesh=mesh,
        in_specs=(wide, rows, rows, rows, wide),
        out_specs=(wide, wide, rows),
        check_vma=False,
    )
```

time: 953 us -> 208 us (0.22)
  waiting for transfers between devices: 544 us -> 0 us
  Pallas kernels: 0 us -> 202 us
  local copies, waits for them, and re-layouts: 193 us -> 5.79 us
  matrix products: 125 us -> 0 us
  other arithmetic: 38.5 us -> 0 us
  starting transfers between devices: 33.8 us -> 0 us
  between operations: 15.1 us -> 0.66 us
    pallas_call x0 -> x2, Pallas kernels: none -> 202 us  [the longest x1 140 us: local(): pl.pallas_call(main_kernel, in_specs=[SM, SM, ANY, ANY, ANY], out_specs=[...]
    reduce_scatter x1 -> x0, waiting for transfers between devices: 172 us -> none  [local(): lax.psum_scatter(lax.dot_general(flat_rows, grad_proj, (((0,), (0,)), (()...]
    ppermute x10 -> x0, waiting for transfers between devices: 162 us -> none  [passed_along(): lax.ppermute(shard, axis, [(i, (i + by) % peers) for i in range(peers)])]
    psum x1 -> x0, waiting for transfers between devices: 114 us -> none  [local(): grad_weight = lax.psum(partial_rows, 'view')]
    all_gather x1 -> x0, waiting for transfers between devices: 94.3 us -> none  [local(): weights = lax.all_gather(w_qkv, 'fsdp', axis=0, tiled=True)]
    dot_general x43 -> x0, matrix products: 87.5 us -> none  [the longest x8 21.2 us: group_step(): jnp.einsum('bhqk,bkhd->bqhd', rounded_probs, value_part, preferred_elemen...]
    while x169 -> x0, local copies, waits for them, and re-layouts: 77.9 us -> none
    dynamic_update_slice x56 -> x0, local copies, waits for them, and re-layouts: 42.4 us -> none  [the longest x8 13.4 us: group_step(): lax.dynamic_update_slice_in_dim(own_grads, grad_k[:, :tokens_view], colum...]
  transfers between devices with their start and end apart: 13 -> 0, of which waited for: 9 -> 0; matrix products, arithmetic and copies ran while one was open for 2% -> 0% of each run, Pallas kernels for 0% -> 0%
where the time goes in v2:
time: 208 us
  Pallas kernels  202 us (97%)
  local copies, waits for them, and re-layouts  5.79 us (3%)
    pallas_call x1, Pallas kernels, local(): pl.pallas_call(main_kernel, in_specs=[SM, SM, ANY, ANY, ANY], out_specs=[...  140 us
    pallas_call x1, Pallas kernels, local(): pl.pallas_call(gather_kernel, in_specs=[ANY] * 3, out_specs=[ANY] * 3, ou...  61.8 us
    unnamed x5, local copies, waits for them, and re-layouts  5.79 us

profile of v2, /device:TPU:1, one launch (start us, length us, event | category | flops | bytes accessed | tf_op | source)
XLA Modules:
  0.0 208.3 jit_solution(3486914122956997213)
XLA Ops:
  0.6 61.8 %shard_map.76 = (bf16[2,8,256,1024]{3,2,1,0:T(8,128)(2,1)}, bf16[1024,1536]{1,0:T(8,128)(2,1)}, bf16[2,512,512]{2,1,0:T(8,128)(2,1)}) custom-call(bf16[2,256,1024]{2,1,0:T(8,128)(2,1)} %bitcast.10, bf16[128,3072]{1,0:T(8,128)(2,1)} %w_ref.1, bf16[2,256,1024]{2,1,0:T(8,128)(2,1)} %bitcast.11), custom_call_target="tpu_custom_call" | custom-call | tf_op jit(solution)/shard_map/pallas_call | solution.py:641
  62.4 140.0 %shard_map.77 = (bf16[2,256,1024]{2,1,0:T(8,128)(2,1)}, f32[128,3072]{1,0:T(8,128)}, bf16[2,256,1024]{2,1,0:T(8,128)(2,1)}) custom-call(s32[16]{0:T(128)} %bitcast.12, s32[8]{0:T(128)} %bitcast.13, bf16[2,2048,1024]{2,1,0:T(8,128)(2,1)} %bitcast.7, bf16[1024,1536]{1,0:T(8,128)(2,1)} %get-tuple-element.10.w_hbm, bf16[2,512,512]{2,1,0:T(8,128)(2,1)} %get-tuple-element.11.g_hbm), custom_call_target="tpu_custom_call" | custom-call | tf_op jit(solution)/shard_map/pallas_call | solution.py:658
  202.5 0.0 copy-start
  202.5 2.4 %copy.11 = bf16[1,1,2,256,1024]{4,3,2,1,0:T(8,128)(2,1)} copy(bf16[1,1,2,256,1024]{4,3,2,1,0:T(8,128)(2,1)} %bitcast.9) | data formatting | bytes 2097152
  204.8 2.3 %copy.12 = bf16[1,1,2,256,1024]{4,3,2,1,0:T(8,128)(2,1)} copy(bf16[1,1,2,256,1024]{4,3,2,1,0:T(8,128)(2,1)} %bitcast.8) | data formatting | bytes 2097152
  207.1 0.0 copy-done
  207.1 1.1 copy.13
Async XLA Ops:
  202.5 4.7 %copy-start = (f32[128,3072]{1,0:T(8,128)S(1)}, f32[128,3072]{1,0:T(8,128)}, u32[]{:S(2)}) copy-start(f32[128,3072]{1,0:T(8,128)} %get-tuple-element.20) | copy-start | bytes 4718596

commit v3 on v2

--- a/solution.py
+++ b/solution.py
@@ -81,117 +81,6 @@
 
 def dot(a, b, dims=NN):
     return lax.dot_general(a, b, dims, preferred_element_type=F32)
-
-def gather_kernel(lat_ref, w_ref, g_ref, lat_all, w_all, g_all, local, send, recv):
-    me = Place()
-    c = me.core
-    rows = w_ref.shape[0]
-    half = w_ref.shape[1] // 6
-    pairs = half // 128
-    samples, toks = lat_ref.shape[0], lat_ref.shape[1]
-    chunks = [(s, pl.ds(t * (toks // 4), toks // 4)) for s in range(samples) for t in range(4)]
-    own_block, other_block = 3 + c, 4 - c
-    strips = []
-    for p in range(pairs):
-        for k in range(3):
-            strips.append(pltpu.make_async_copy(
-                w_ref.at[:, at((2 * k + c) * half + p * 128, 128)],
-                w_all.at[at(me.fsdp * rows, rows), pl.ds((3 * p + k) * 128, 128)],
-                local.at[3 * p + k]))
-    kept = []
-    base = 3 * pairs
-    for s in range(samples):
-        kept.append(pltpu.make_async_copy(lat_ref.at[s], lat_all.at[s, own_block], local.at[base + s]))
-        kept.append(pltpu.make_async_copy(
-            g_ref.at[s, :, at(c * half, half)], g_all.at[s, at(c * toks, toks), :], local.at[base + 2 + s]))
-    for copy in strips + kept:
-        copy.start()
-    greet((me.up, me.down, me.pair, me.mate, me.z_up, me.z_down, me.outer))
-    mail = Mail(send, recv)
-    remote = mail.copy
-
-    def block(b, chunk):
-        s, t = chunk
-        return lat_all.at[s, b, t]
-
-    def shard(f, part=None):
-        if part is None:
-            return w_all.at[at(f * rows, rows)]
-        return w_all.at[at(f * rows + part * (rows // 2), rows // 2)]
-
-    n = range(len(chunks))
-    mine = [lat_ref.at[s, t] for s, t in chunks]
-    up = [remote(mine[i], block(1 + c, chunks[i]), me.up) for i in n]
-    down = [remote(mine[i], block(5 + c, chunks[i]), me.down) for i in n]
-    up_far = [mail.again(i, block(7 * c, chunks[i]), block(1 + c, chunks[i]), me.up) for i in n]
-    down_far = [mail.again(len(chunks) + i, block(7 * c, chunks[i]), block(5 + c, chunks[i]), me.down) for i in n]
-    to_pair = [remote(mine[i], block(7 * c, chunks[i]), me.pair) for i in n]
-    to_mate = [remote(lat_ref.at[s], lat_all.at[s, own_block], me.mate) for s in range(samples)]
-    relays = {b: [remote(lat_all.at[s, bb], lat_all.at[s, bb], me.mate) for s in range(samples)]
-              for b, bb in (("pair", 7 * c), ("up", 1 + c), ("down", 5 + c))}
-    g_mate = [remote(
-        g_ref.at[s, :, at((1 - c) * half, half)], g_all.at[s, at(c * toks, toks), :], me.mate) for s in range(samples)]
-    first, last = me.y == 0, me.y == me.ys - 1
-    f0, f_up, f_down, f_out, far = me.fsdp, me.f_up, me.f_down, me.f_outer, me.f_far
-    w_up = remote(shard(f0), shard(f0), me.z_up)
-    w_down = remote(shard(f0), shard(f0), me.z_down)
-    w_out = remote(shard(f0), shard(f0), me.outer)
-    w_up2 = remote(shard(f_down, 0), shard(f_down, 0), me.z_up)
-    w_down2 = remote(shard(f_up, 1), shard(f_up, 1), me.z_down)
-    o_up = remote(shard(f_out), shard(f_out), me.z_up)
-    o_down = remote(shard(f_out), shard(f_out), me.z_down)
-    o_far = [remote(shard(far, part), shard(far, part), me.outer) for part in range(2)]
-
-    to_pair[0].start()
-    to_pair[1].start()
-    for copy in strips:
-        copy.wait()
-    w_up.start()
-    w_down.start()
-    w_out.start()
-    for i in n:
-        pl.when(jnp.logical_not(last))(up[i].start)
-        pl.when(jnp.logical_not(first))(down[i].start)
-    for copy in to_mate + g_mate:
-        copy.start()
-    for i in n:
-        to_pair[i].wait_send()
-        if i + 2 < len(chunks):
-            to_pair[i + 2].start()
-        to_pair[i].wait_recv()
-        pl.when(last)(up_far[i].start)
-        pl.when(first)(down_far[i].start)
-        if i == len(chunks) // 2 - 1:
-            relays["pair"][0].start()
-        if i == 2:
-            w_up.wait_recv()
-            w_up2.start()
-            w_down.wait_recv()
-            w_down2.start()
-            w_out.wait_recv()
-            o_up.start()
-            o_down.start()
-        if i == 5:
-            w_up2.wait_recv()
-            o_far[0].start()
-            w_down2.wait_recv()
-            o_far[1].start()
-    relays["pair"][1].start()
-    each = len(chunks) // samples
-    for s in range(samples):
-        for i in range(s * each, (s + 1) * each):
-            up[i].wait_recv()
-        relays["up"][s].start()
-        for i in range(s * each, (s + 1) * each):
-            down[i].wait_recv()
-        relays["down"][s].start()
-    for copy in (o_up, o_down, *o_far, *to_mate, *g_mate, *relays["pair"], *relays["up"], *relays["down"]):
-        copy.wait_recv()
-    for i, copy in enumerate(mail.sent):
-        if not 2 * len(chunks) <= i < 3 * len(chunks):
-            copy.wait_send()
-    for copy in kept:
-        copy.wait()
 
 
 def when(condition):
@@ -315,18 +204,32 @@
 KINDS = ("a1u", "a1d", "bx", "a2u", "a2d", "b1u", "b1d", "ax", "b2u", "b2d", "p1", "r0", "r1", "r2", "g0", "g1", "g2", "pb", "ma", "mb")
 
 
+def sample_and_pair(t):
+    if isinstance(t, int):
+        return (t // 2, t % 2) if t < 4 else (t % 2, t // 2)
+    early = t < 4
+    return jnp.where(early, t // 2, t % 2), jnp.where(early, t % 2, t // 2)
+
+
 def main_kernel(cycle_ref, cross_ref, lat_hbm, w_hbm, g_hbm, att_full, dw_out, dl_out,
                 lat, w, g, k_s, v_s, q_s, st, pb, gs, att, own, out, inbox, gp, dwb, dl_out_s, dl_in,
                 z1u, z1d, z2u, z2d, su, sd, zs, xin, xain, xa, q1u, q1d, q2u, q2d, qsu, qsd,
                 whole, v1, vsum, v2, fin, fing, mate_in,
-                local, tsend, trecv, rsend, rrecv, dsend, drecv):
+                local, tsend, trecv, rsend, rrecv, dsend, drecv, gsend, grecv):
     me = Place()
     c, y, z, xh, xl = me.core, me.y, me.z, me.x_hi, me.x_lo
     zu, zd, zf = (z + 1) % 4, (z + 3) % 4, (z + 2) % 4
     width = 512
-    loads = [pltpu.make_async_copy(w_hbm, w, local.at[0]), pltpu.make_async_copy(lat_hbm.at[0], lat.at[0], local.at[1]),
-             pltpu.make_async_copy(g_hbm, g, local.at[2]), pltpu.make_async_copy(lat_hbm.at[1], lat.at[1], local.at[3])]
-    for copy in loads:
+    strips, kept = [], []
+    for p in range(4):
+        for k in range(3):
+            strips.append(pltpu.make_async_copy(
+                w_hbm.at[:, at((2 * k + c) * width + p * 128, 128)],
+                w.at[at(me.fsdp * 128, 128), pl.ds((3 * p + k) * 128, 128)], local.at[3 * p + k]))
+    for s in range(2):
+        kept.append(pltpu.make_async_copy(lat_hbm.at[s], lat.at[s, at((3 + c) * TOK, TOK)], local.at[12 + s]))
+        kept.append(pltpu.make_async_copy(g_hbm.at[s, :, at(c * width, width)], g.at[s, at(c * TOK, TOK)], local.at[14 + s]))
+    for copy in strips + kept:
         copy.start()
     greet((me.up, me.down, me.over, me.pair, me.mate, me.z_up, me.z_down, me.outer))
 
@@ -361,15 +264,15 @@
         return mail(out.at[t % 3, 2], inbox.at[t, 2], tsend.at[2, t % 3], trecv.at[2, t], me.pair)
 
     def columns(t):
-        return at(c * width + (t // 2) * 128, 128)
+        return at(c * width + sample_and_pair(t)[1] * 128, 128)
 
     def att_mate(t):
-        return mail(att.at[t % 3, at((1 - c) * TOK, TOK)], att_full.at[t % 2, :, columns(t)],
+        return mail(att.at[t % 3, at((1 - c) * TOK, TOK)], att_full.at[sample_and_pair(t)[0], :, columns(t)],
                     tsend.at[3, t % 3], trecv.at[3, t], me.mate)
 
     def att_own(t):
         return pltpu.make_async_copy(
-            att.at[t % 3, at(c * TOK, TOK)], att_full.at[t % 2, :, columns(t)], tsend.at[4, t % 3])
+            att.at[t % 3, at(c * TOK, TOK)], att_full.at[sample_and_pair(t)[0], :, columns(t)], tsend.at[4, t % 3])
 
     def red(kind, p, src, dst, to):
         i = KINDS.index(kind)
@@ -509,10 +412,11 @@
         mate_other(p).start()
 
     phases = (phase1, phase2, phase3, phase4, phase5, phase6, phase7, phase8)
+    begins = (4, 5, 7, 9)
 
     def gather_grads(t):
         across(t).wait_recv()
-        s, p = t % 2, t // 2
+        s, p = sample_and_pair(t)
         for i in range(2):
             total = own[t % 3, i] + f32(inbox[t, 2, i]) + f32(inbox[t, 1, i]) * keep_down + f32(inbox[t, 0, i]) * keep_up
             gp[p, at(s * 512, 512), (1 + i) * 128:(2 + i) * 128] = total.astype(BF)
@@ -537,21 +441,133 @@
                 across(u).start()
 
         when(both(t >= 2, t <= STEPS + 1))(lambda: gather_grads(t - 2))
-        for k, phase in enumerate(phases):
-            if isinstance(t, int) or k < 5:
-                due = t - 3 - k
-                when(both(due >= 0, due <= 6, due % 2 == 0))(lambda: phase(due // 2))
-
-    loads[0].wait()
-    loads[1].wait()
-    loads[2].wait()
+        for p, begin in reversed(list(enumerate(begins))):
+            for k, phase in enumerate(phases):
+                if isinstance(t, int) or begin + k < STEPS:
+                    when(t == begin + k)(functools.partial(phase, p))
+
+    sent = []
+    slots = iter(range(64))
+
+    def post(src, dst, to, own=None):
+        i = next(slots)
+        made = mail(src, dst, gsend.at[i], grecv.at[i], to)
+        sent.append(made)
+        return made if own is None else (made, mail(own, dst, gsend.at[i], grecv.at[i], to))
+
+    def rows_at(s, b, start=0, size=TOK):
+        return lat.at[s, at(b * TOK + start, size)]
+
+    def w_at(f, group, start=0, size=128):
+        return w.at[at(f * 128 + start, size), pl.ds(group * 768, 768)]
+
+    cuts = {0: [(i * 64, 64) for i in range(4)], 1: [(0, TOK)]}
+    to_pair, to_up, to_down, to_mate, relays, g_mate = {}, {}, {}, {}, {}, []
+    for s in range(2):
+        to_pair[s] = [post(lat_hbm.at[s, pl.ds(*cut)], rows_at(s, 7 * c, *cut), me.pair) for cut in cuts[s]]
+        to_up[s] = [post(rows_at(s, 7 * c, *cut), rows_at(s, 1 + c, *cut), me.up, lat_hbm.at[s, pl.ds(*cut)]) for cut in cuts[s]]
+        to_down[s] = [post(rows_at(s, 7 * c, *cut), rows_at(s, 5 + c, *cut), me.down, lat_hbm.at[s, pl.ds(*cut)]) for cut in cuts[s]]
+        to_mate[s] = post(lat_hbm.at[s], rows_at(s, 3 + c), me.mate)
+        relays[s] = [post(rows_at(s, b), rows_at(s, b), me.mate) for b in (7 * c, 1 + c, 5 + c)]
+        g_mate.append(post(g_hbm.at[s, :, at((1 - c) * width, width)], g.at[s, at(c * TOK, TOK)], me.mate))
+    f0, f_up, f_down, f_out, far = me.fsdp, me.f_up, me.f_down, me.f_outer, me.f_far
+    w_mail = [dict(
+        up=post(w_at(f0, grp), w_at(f0, grp), me.z_up),
+        down=post(w_at(f0, grp), w_at(f0, grp), me.z_down),
+        out=post(w_at(f0, grp), w_at(f0, grp), me.outer),
+        up2=post(w_at(f_down, grp, 0, 64), w_at(f_down, grp, 0, 64), me.z_up),
+        down2=post(w_at(f_up, grp, 64, 64), w_at(f_up, grp, 64, 64), me.z_down),
+        out_up=post(w_at(f_out, grp), w_at(f_out, grp), me.z_up),
+        out_down=post(w_at(f_out, grp), w_at(f_out, grp), me.z_down),
+        far0=post(w_at(far, grp, 0, 64), w_at(far, grp, 0, 64), me.outer),
+        far1=post(w_at(far, grp, 64, 64), w_at(far, grp, 64, 64), me.outer),
+    ) for grp in range(2)]
+
+    def w_first(grp):
+        for copy in strips[6 * grp:6 * grp + 6]:
+            copy.wait()
+        for name in ("up", "down", "out"):
+            w_mail[grp][name].start()
+
+    def w_second(grp):
+        m = w_mail[grp]
+        m["up"].wait_recv()
+        m["up2"].start()
+        m["down"].wait_recv()
+        m["down2"].start()
+        m["out"].wait_recv()
+        m["out_up"].start()
+        m["out_down"].start()
+
+    def w_third(grp):
+        m = w_mail[grp]
+        m["up2"].wait_recv()
+        m["far0"].start()
+        m["down2"].wait_recv()
+        m["far1"].start()
+
+    def w_last(grp):
+        for name in ("out_up", "out_down", "far0", "far1"):
+            w_mail[grp][name].wait_recv()
+
+    def lat_first(s):
+        for i in range(len(cuts[s])):
+            pl.when(jnp.logical_not(last))(to_up[s][i][1].start)
+            pl.when(jnp.logical_not(first))(to_down[s][i][1].start)
+        to_mate[s].start()
+        g_mate[s].start()
+
+    def lat_wrap(s, i):
+        to_pair[s][i].wait_recv()
+        pl.when(last)(to_up[s][i][0].start)
+        pl.when(first)(to_down[s][i][0].start)
+
+    def lat_relay(s):
+        for i in range(len(cuts[s])):
+            to_up[s][i][0].wait_recv()
+        relays[s][1].start()
+        for i in range(len(cuts[s])):
+            to_down[s][i][0].wait_recv()
+        relays[s][2].start()
+
+    def lat_last(s):
+        for copy in (to_mate[s], g_mate[s], *relays[s]):
+            copy.wait_recv()
+
+    chunks = len(cuts[0])
+    to_pair[0][0].start()
+    to_pair[0][1].start()
+    w_first(0)
+    lat_first(0)
+    for i in range(chunks):
+        to_pair[0][i].wait_send()
+        if i + 2 < chunks:
+            to_pair[0][i + 2].start()
+        lat_wrap(0, i)
+        if i == 1:
+            w_second(0)
+        if i == 2:
+            w_third(0)
+    relays[0][0].start()
+    to_pair[1][0].start()
+    lat_relay(0)
+    w_first(1)
+    lat_first(1)
+    w_last(0)
+    for copy in kept:
+        copy.wait()
+    lat_last(0)
 
     def step(t, carry):
-        s, p = t % 2, t // 2
-
-        @pl.when(t == 1)
+        s, p = sample_and_pair(t)
+
+        @pl.when(t == 2)
         def _():
-            loads[3].wait()
+            lat_last(1)
+
+        @pl.when(t == 4)
+        def _():
+            w_last(1)
 
         @pl.when(t >= 3)
         def _():
@@ -574,6 +590,18 @@
 
         att_mate(t).start()
         att_own(t).start()
+
+        @pl.when(t == 0)
+        def _():
+            lat_wrap(1, 0)
+            relays[1][0].start()
+            w_second(1)
+
+        @pl.when(t == 1)
+        def _():
+            lat_relay(1)
+            w_third(1)
+
         service(t)
         return carry
 
@@ -628,6 +656,9 @@
             make(p).wait_send()
         for copy in ring(p) + back(p):
             copy.wait_send()
+    for i, copy in enumerate(sent):
+        if i >= chunks:
+            copy.wait_send()
 
 
 def local(latents, w_qkv, cycle_links, cross_links, d_attended):
@@ -637,20 +668,6 @@
     ANY = pl.BlockSpec(memory_space=pl.ANY)
     VM = pl.BlockSpec(memory_space=pltpu.VMEM)
     SM = pl.BlockSpec(memory_space=pltpu.SMEM)
-    n = 48
-    lat_all, w_all, g_all = pl.pallas_call(
-        gather_kernel,
-        in_specs=[ANY] * 3,
-        out_specs=[ANY] * 3,
-        out_shape=[
-            jax.ShapeDtypeStruct((samples, 8, toks, model), BF),
-            jax.ShapeDtypeStruct((model, wide // 2), BF),
-            jax.ShapeDtypeStruct((samples, 2 * toks, half), BF),
-        ],
-        scratch_shapes=[pltpu.SemaphoreType.DMA((16,)), pltpu.SemaphoreType.DMA((n,)), pltpu.SemaphoreType.DMA((n,))],
-        compiler_params=pltpu.CompilerParams(collective_id=0, has_side_effects=True, vmem_limit_bytes=VMEM_LIMIT),
-    )(latents[0, 0], w_qkv, d_attended[0, 0])
-
     def vm(*shape, dtype=BF):
         return pltpu.VMEM(shape, dtype)
 
@@ -678,13 +695,14 @@
             vm(4, 32, W), vm(4, 32, W),
             vm(4, 64, W), vm(4, 64, W), vm(4, 64, W), vm(4, 64, W),
             vm(4, rows, W), vm(4, 64, W), vm(4, 64, W), vm(4, 3, 16, W), vm(4, 16, W), vm(4, rows, W), vm(4, rows, W),
-            pltpu.SemaphoreType.DMA((4,)),
+            pltpu.SemaphoreType.DMA((16,)),
             pltpu.SemaphoreType.DMA((5, 3)), pltpu.SemaphoreType.DMA((4, STEPS)),
             pltpu.SemaphoreType.DMA((len(KINDS), 4)), pltpu.SemaphoreType.DMA((len(KINDS), 4)),
             pltpu.SemaphoreType.DMA((1,)), pltpu.SemaphoreType.DMA((1,)),
+            pltpu.SemaphoreType.DMA((64,)), pltpu.SemaphoreType.DMA((64,)),
         ],
-        compiler_params=pltpu.CompilerParams(collective_id=1, has_side_effects=True, vmem_limit_bytes=63 * 2**20),
-    )(cycle_links[0], cross_links[0], lat_all.reshape(samples, 8 * toks, model), w_all, g_all)
+        compiler_params=pltpu.CompilerParams(collective_id=0, has_side_effects=True, vmem_limit_bytes=63 * 2**20),
+    )(cycle_links[0], cross_links[0], latents[0, 0], w_qkv, d_attended[0, 0])
     return att_full[None, None], dl_out[None, None], dw_out
 
 

time: 208 us -> 176 us (0.85)
  Pallas kernels: 202 us -> 171 us
    pallas_call x1 -> x0, Pallas kernels: 61.8 us -> none  [local(): pl.pallas_call(gather_kernel, in_specs=[ANY] * 3, out_specs=[ANY] * 3, ou...]
    pallas_call x1, Pallas kernels: 140 us -> 171 us  [local(): pl.pallas_call(main_kernel, in_specs=[SM, SM, ANY, ANY, ANY], out_specs=[...]
    unnamed x5 -> x7, local copies, waits for them, and re-layouts: 5.79 us -> 4.54 us
where the time goes in v3:
time: 176 us
  Pallas kernels  171 us (97%)
  local copies, waits for them, and re-layouts  4.54 us (3%)
    pallas_call x1, Pallas kernels, local(): pl.pallas_call(main_kernel, in_specs=[SM, SM, ANY, ANY, ANY], out_specs=[...  171 us
    unnamed x7, local copies, waits for them, and re-layouts  4.54 us

profile of v3, /device:TPU:1, one launch (start us, length us, event | category | flops | bytes accessed | tf_op | source)
XLA Modules:
  0.0 176.0 jit_solution(16100275618563971957)
XLA Ops:
  0.6 170.8 %shard_map.76 = (bf16[2,256,1024]{2,1,0:T(8,128)(2,1)}, f32[128,3072]{1,0:T(8,128)}, bf16[2,256,1024]{2,1,0:T(8,128)(2,1)}) custom-call(s32[16]{0:T(128)} %bitcast.10, s32[8]{0:T(128)} %bitcast.11, bf16[2,256,1024]{2,1,0:T(8,128)(2,1)} %bitcast.6, bf16[128,3072]{1,0:T(8,128)(2,1)} %w_hbm.1, bf16[2,256,1024]{2,1,0:T(8,128)(2,1)} %bitcast.7), custom_call_target="tpu_custom_call" | custom-call | tf_op jit(solution)/shard_map/pallas_call | solution.py:675
  171.5 0.0 copy-start.1
  171.5 0.0 copy-start
  171.5 2.4 %copy.11 = bf16[1,1,2,256,1024]{4,3,2,1,0:T(8,128)(2,1)} copy(bf16[1,1,2,256,1024]{4,3,2,1,0:T(8,128)(2,1)} %bitcast.9) | data formatting | bytes 2097152
  173.9 0.0 copy-done.1
  173.9 1.0 copy.12
  174.9 0.0 copy-done
  174.9 1.1 copy.13
Async XLA Ops:
  171.5 2.4 %copy-start.1 = (bf16[2,256,1024]{2,1,0:T(8,128)(2,1)S(1)}, bf16[2,256,1024]{2,1,0:T(8,128)(2,1)}, u32[]{:S(2)}) copy-start(bf16[2,256,1024]{2,1,0:T(8,128)(2,1)} %get-tuple-element.7) | copy-start | bytes 3145732
  171.5 3.4 %copy-start = (f32[128,3072]{1,0:T(8,128)S(1)}, f32[128,3072]{1,0:T(8,128)}, u32[]{:S(2)}) copy-start(f32[128,3072]{1,0:T(8,128)} %get-tuple-element.14) | copy-start | bytes 4718596

commit v4 on v3

--- a/solution.py
+++ b/solution.py
@@ -96,67 +96,97 @@
     return functools.reduce(jnp.logical_and, conditions) if conditions else True
 
 
-def view_pass(bias, q, g, k_rows, v_rows, kt, vt, gt, st, pb, gs):
-    lane = lax.broadcasted_iota(jnp.int32, (1, 128), 1)
-    outs, dqs, qms, gms = [], [], [], []
-    for h in range(2):
-        mine = (lane >= 64) if h else (lane < 64)
-        qm = jnp.where(mine, q, jnp.zeros_like(q))
-        gm = jnp.where(mine, g, jnp.zeros_like(g))
-        qms.append(qm)
-        gms.append(gm)
-        tops = []
-        for j in range(6):
-            rows = pl.ds(j * TOK, TOK)
-            s = dot(k_rows(j), qm, NT)
-            st[h, rows, :] = s
-            tops.append(jnp.max(s, axis=0, keepdims=True) * (SCALE * LOG2E) + bias[j])
-        top = functools.reduce(jnp.maximum, tops)
-        total = jnp.zeros((1, TOK), F32)
-        for j in range(6):
-            rows = pl.ds(j * TOK, TOK)
-            e = jnp.exp2(st[h, rows, :] * (SCALE * LOG2E) - (top - bias[j]))
-            st[h, rows, :] = e
-            total = total + jnp.sum(e, axis=0, keepdims=True)
-        inv = 1.0 / total
-        for j in range(6):
-            rows = pl.ds(j * TOK, TOK)
-            p = st[h, rows, :] * inv
-            st[h, rows, :] = p
-            pb[rows, h * TOK:(h + 1) * TOK] = p.astype(BF)
-        ot = dot(vt, pb[:, h * TOK:(h + 1) * TOK])[h * 64:(h + 1) * 64]
-        outs.append(ot)
-        delta = jnp.sum(gt[h * 64:(h + 1) * 64] * ot, axis=0, keepdims=True)
-        for j in range(6):
-            rows = pl.ds(j * TOK, TOK)
-            d = dot(v_rows(j), gm, NT)
-            gs[rows, h * TOK:(h + 1) * TOK] = (st[h, rows, :] * (d - delta)).astype(BF)
-        dqs.append(dot(kt, gs[:, h * TOK:(h + 1) * TOK])[h * 64:(h + 1) * 64])
-    return (
-        jnp.concatenate(outs, axis=0),
-        jnp.concatenate(dqs, axis=0) * SCALE,
-        jnp.concatenate(qms, axis=0),
-        jnp.concatenate(gms, axis=0),
-    )
+def head_pass(view, h, bias, qt, gt, k_rows, v_rows, kt, vt, st, pb, gs, att_t, dq_t, own, term):
+    head = slice(h * 64, (h + 1) * 64)
+    row = lax.broadcasted_iota(jnp.int32, (128, 1), 0)
+    mine = (row >= 64) if h else (row < 64)
+    qm = jnp.where(mine, qt, jnp.zeros_like(qt)).astype(BF)
+    gm = jnp.where(mine, gt, jnp.zeros_like(gt)).astype(BF)
+    cols = slice(h * TOK, (h + 1) * TOK)
+    blocks = [pl.ds(j * TOK, TOK) for j in range(6)]
+    tops = []
+    for j in range(0, 6, SPAN):
+        s = dot(k_rows(j, SPAN), qm)
+        for i in range(SPAN):
+            part = s[i * TOK:(i + 1) * TOK]
+            st[h, blocks[j + i], :] = part
+            tops.append(jnp.max(part, axis=0, keepdims=True) * (SCALE * LOG2E) + bias[j + i])
+            yield
+    top = functools.reduce(jnp.maximum, tops)
+    total = jnp.zeros((1, TOK), F32)
+    for j, rows in enumerate(blocks):
+        e = jnp.exp2(st[h, rows, :] * (SCALE * LOG2E) - (top - bias[j]))
+        st[h, rows, :] = e
+        total = total + jnp.sum(e, axis=0, keepdims=True)
+        yield
+    inv = 1.0 / total
+    for rows in blocks:
+        pb[rows, cols] = (st[h, rows, :] * inv).astype(BF)
+        yield
+    ot = dot(vt()[head], pb[:, cols])
+    att_t[h] = ot
+    delta = jnp.sum(gt[head] * ot, axis=0, keepdims=True)
+    yield
+    for j in range(0, 6, SPAN):
+        d = dot(v_rows(j, SPAN), gm)
+        for i in range(SPAN):
+            part = d[i * TOK:(i + 1) * TOK]
+            gs[blocks[j + i], cols] = (st[h, blocks[j + i], :] * inv * (part - delta)).astype(BF)
+            yield
+    dq_t[h] = dot(kt()[head], gs[:, cols]) * SCALE
+    yield
+    q_head, g_head = qt[head].astype(BF), gt[head].astype(BF)
+    for j, rows in enumerate(blocks):
+        b = j + 2 * view
+        grads = dot(q_head, gs[rows, cols], NT) * SCALE, dot(g_head, pb[rows, cols], NT)
+        for i, grad in enumerate(grads):
+            if b in (3, 4):
+                w = pl.ds((b - 3) * TOK, TOK)
+                grad = grad if b - 3 == view else grad.astype(BF).astype(F32)
+                own[i, head, w] = grad if view == 0 else own[i, head, w] + grad
+            else:
+                n, w = {0: (2, 0), 1: (0, 0), 2: (0, 1), 5: (1, 0), 6: (1, 1), 7: (2, 1)}[b]
+                w = pl.ds(w * TOK, TOK)
+                grad = grad.astype(BF)
+                if b in (2, 5) and view == 1:
+                    grad = (term[n, i, head, w].astype(F32) + grad.astype(F32)).astype(BF)
+                term[n, i, head, w] = grad
+        yield
 
 
 def project(lat, w, s, p, k_s, v_s, q_s):
-    span = 2 * lat.shape[1] // 8
-    first = 3 * span // 2
-    w_kv = w[:, at(p * 384 + 128, 128)], w[:, at(p * 384 + 256, 128)]
-    w_kv = jnp.concatenate(w_kv, axis=1)
+    span = PROJECT_ROWS
+    first, count = 3 * lat.shape[1] // 8, lat.shape[1] // 4
+    w_kv = w[:, pl.ds(pl.multiple_of(p * 384 + 128, 128), 256)]
     for r in range(lat.shape[1] // span):
         rows = pl.ds(r * span, span)
         kv = dot(lat[s, rows, :], w_kv).astype(BF)
         k_s[rows, :] = kv[:, :128]
         v_s[rows, :] = kv[:, 128:]
-    q_s[...] = dot(lat[s, pl.ds(first, span), :], w[:, at(p * 384, 128)]).astype(BF)
-
-
-def attend(bias, s, p, g_ref, k_s, v_s, q_s, st, pb, gs, att, dq, own, term):
+        yield
+    q_s[...] = dot(lat[s, pl.ds(first, count), :], w[:, at(p * 384, 128)]).astype(BF)
+    yield
+
+
+def weave(threads):
+    threads = list(threads)
+    tick = 0
+    while threads:
+        for thread in list(threads):
+            start, every, work = thread
+            if tick >= start and (tick - start) % every == 0:
+                try:
+                    next(work)
+                except StopIteration:
+                    threads.remove(thread)
+        tick += 1
+
+
+def attend(bias, s, p, g_ref, k_s, v_s, q_s, st, pb, gs, att, dq, own, term, beside=()):
     kt = k_s[...].T
     vt = v_s[...].T
-    held = []
+    threads = list(beside)
+    results = []
     for view in range(2):
         rows = pl.ds(view * TOK, TOK)
         q = q_s[rows, :]
@@ -164,42 +194,24 @@
         gt = g.astype(F32).T
         span = slice(2 * view * TOK, (2 * view + 6) * TOK)
 
+        qt = q.astype(F32).T
+
         def rows_of(ref, view=view):
-            return lambda j: ref[pl.ds((2 * view + j) * TOK, TOK), :]
-
-        ot, dqt, qm, gm = view_pass(
-            bias[view], q, g, rows_of(k_s), rows_of(v_s), kt[:, span], vt[:, span], gt,
-            st.at[view], pb.at[view], gs.at[view])
-        att[rows, :] = ot.T.astype(BF)
-        dq[rows, :] = dqt.T.astype(BF)
-        held.append((qm, gm))
-    for b in range(8):
-        parts = []
-        for view in range(2):
-            j = b - 2 * view
-            if 0 <= j < 6:
-                qm, gm = held[view]
-                rows = pl.ds(j * TOK, TOK)
-                dk = dot(gs[view, rows, :], qm) * SCALE
-                dv = dot(pb[view, rows, :], gm)
-                parts.append((dk, dv))
-        dk, dv = parts[0]
-        if b in (3, 4):
-            w = b - 3
-            mine, other = parts[w], parts[1 - w]
-            rows = pl.ds(w * TOK, TOK)
-            own[0, rows, :] = mine[0] + other[0].astype(BF).astype(F32)
-            own[1, rows, :] = mine[1] + other[1].astype(BF).astype(F32)
-        else:
-            if len(parts) == 2:
-                dk = dk.astype(BF).astype(F32) + parts[1][0].astype(BF).astype(F32)
-                dv = dv.astype(BF).astype(F32) + parts[1][1].astype(BF).astype(F32)
-            n, w = {0: (2, 0), 1: (0, 0), 2: (0, 1), 5: (1, 0), 6: (1, 1), 7: (2, 1)}[b]
-            rows = pl.ds(w * TOK, TOK)
-            term[n, 0, rows, :] = dk.astype(BF)
-            term[n, 1, rows, :] = dv.astype(BF)
-
-
+            return lambda j, n: ref[pl.ds((2 * view + j) * TOK, n * TOK), :]
+
+        att_t, dq_t = {}, {}
+        results.append((rows, att_t, dq_t))
+        for h in range(2):
+            threads.append((OFFSET * (2 * view + h), 1, head_pass(
+                view, h, bias[view], qt, gt, rows_of(k_s), rows_of(v_s), lambda span=span: kt[:, span],
+                lambda span=span: vt[:, span], st.at[view], pb.at[view], gs.at[view], att_t, dq_t, own, term)))
+    weave(threads)
+    for rows, att_t, dq_t in results:
+        att[rows, :] = jnp.concatenate([att_t[0], att_t[1]], axis=0).T.astype(BF)
+        dq[rows, :] = jnp.concatenate([dq_t[0], dq_t[1]], axis=0).T.astype(BF)
+
+
+OFFSET, SPAN, PROJECT_ROWS = 9, 1, 512
 STEPS = 8
 KINDS = ("a1u", "a1d", "bx", "a2u", "a2d", "b1u", "b1d", "ax", "b2u", "b2d", "p1", "r0", "r1", "r2", "g0", "g1", "g2", "pb", "ma", "mb")
 
@@ -419,7 +431,7 @@
         s, p = sample_and_pair(t)
         for i in range(2):
             total = own[t % 3, i] + f32(inbox[t, 2, i]) + f32(inbox[t, 1, i]) * keep_down + f32(inbox[t, 0, i]) * keep_up
-            gp[p, at(s * 512, 512), (1 + i) * 128:(2 + i) * 128] = total.astype(BF)
+            gp[p, at(s * 512, 512), (1 + i) * 128:(2 + i) * 128] = total.T.astype(BF)
 
     def service(t):
         @when(both(t >= 1, t <= STEPS))
@@ -558,14 +570,21 @@
         copy.wait()
     lat_last(0)
 
+    def projected(t, slot):
+        for _ in project(lat, w, *sample_and_pair(t), k_s.at[slot], v_s.at[slot], q_s.at[slot]):
+            pass
+
+    projected(0, 0)
+
     def step(t, carry):
         s, p = sample_and_pair(t)
 
         @pl.when(t == 2)
         def _():
             lat_last(1)
-
-        @pl.when(t == 4)
+            projected(2, 0)
+
+        @pl.when(t == 3)
         def _():
             w_last(1)
 
@@ -578,9 +597,11 @@
             att_mate(u).wait_send()
             att_own(u).wait()
 
-        project(lat, w, s, p, k_s, v_s, q_s)
-        attend(bias, s, p, g, k_s, v_s, q_s, st, pb, gs, att.at[t % 3], gp.at[p, at(s * 512, 512), pl.ds(0, 128)],
-               own.at[t % 3], out.at[t % 3])
+        now, later = t % 2, (t + 1) % 2
+        s_next, p_next = sample_and_pair(jnp.where(t == 1, 1, jnp.minimum(t + 1, STEPS - 1)))
+        beside = project(lat, w, s_next, p_next, k_s.at[later], v_s.at[later], q_s.at[later])
+        attend(bias, s, p, g, k_s.at[now], v_s.at[now], q_s.at[now], st, pb, gs, att.at[t % 3],
+               gp.at[p, at(s * 512, 512), pl.ds(0, 128)], own.at[t % 3], out.at[t % 3], [(4, 2, beside)])
         up(t).start()
         down(t).start()
 
@@ -683,10 +704,10 @@
         ],
         scratch_shapes=[
             vm(samples, 8 * toks, model), vm(model, wide // 2), vm(samples, 2 * toks, half),
-            vm(8 * toks, 128), vm(8 * toks, 128), vm(2 * toks, 128),
+            vm(2, 8 * toks, 128), vm(2, 8 * toks, 128), vm(2, 2 * toks, 128),
             vm(2, 2, 6 * toks, toks, dtype=F32), vm(2, 6 * toks, 2 * toks), vm(2, 6 * toks, 2 * toks),
-            vm(3, 2 * toks, 128), vm(3, 2, 2 * toks, 128, dtype=F32),
-            vm(3, 3, 2, 2 * toks, 128), vm(STEPS, 3, 2, 2 * toks, 128),
+            vm(3, 2 * toks, 128), vm(3, 2, 128, 2 * toks, dtype=F32),
+            vm(3, 3, 2, 128, 2 * toks), vm(STEPS, 3, 2, 128, 2 * toks),
             vm(4, samples * 2 * toks, W), vm(4, 2, 4, rows, W),
             vm(samples, toks, model), vm(samples, toks, model),
             vm(4, 2, 32, W), vm(4, 2, 32, W),

time: 176 us -> 158 us (0.90)
  Pallas kernels: 171 us -> 152 us
    pallas_call x1, Pallas kernels: 171 us -> 152 us  [local(): pl.pallas_call(main_kernel, in_specs=[SM, SM, ANY, ANY, ANY], out_specs=[...]
where the time goes in v4:
time: 158 us
  Pallas kernels  152 us (96%)
  local copies, waits for them, and re-layouts  4.54 us (3%)
    pallas_call x1, Pallas kernels, local(): pl.pallas_call(main_kernel, in_specs=[SM, SM, ANY, ANY, ANY], out_specs=[...  152 us
    unnamed x7, local copies, waits for them, and re-layouts  4.54 us

profile of v4, /device:TPU:1, one launch (start us, length us, event | category | flops | bytes accessed | tf_op | source)
XLA Modules:
  0.0 157.7 jit_solution(887874892867973639)
XLA Ops:
  0.6 152.5 %shard_map.76 = (bf16[2,256,1024]{2,1,0:T(8,128)(2,1)}, f32[128,3072]{1,0:T(8,128)}, bf16[2,256,1024]{2,1,0:T(8,128)(2,1)}) custom-call(s32[16]{0:T(128)} %bitcast.10, s32[8]{0:T(128)} %bitcast.11, bf16[2,256,1024]{2,1,0:T(8,128)(2,1)} %bitcast.6, bf16[128,3072]{1,0:T(8,128)(2,1)} %w_hbm.1, bf16[2,256,1024]{2,1,0:T(8,128)(2,1)} %bitcast.7), custom_call_target="tpu_custom_call" | custom-call | tf_op jit(solution)/shard_map/pallas_call | solution.py:696
  153.1 0.0 copy-start.1
  153.1 0.0 copy-start
  153.1 2.4 %copy.11 = bf16[1,1,2,256,1024]{4,3,2,1,0:T(8,128)(2,1)} copy(bf16[1,1,2,256,1024]{4,3,2,1,0:T(8,128)(2,1)} %bitcast.9) | data formatting | bytes 2097152
  155.5 0.0 copy-done.1
  155.5 1.0 copy.12
  156.5 0.0 copy-done
  156.5 1.1 copy.13
Async XLA Ops:
  153.1 2.4 %copy-start.1 = (bf16[2,256,1024]{2,1,0:T(8,128)(2,1)S(1)}, bf16[2,256,1024]{2,1,0:T(8,128)(2,1)}, u32[]{:S(2)}) copy-start(bf16[2,256,1024]{2,1,0:T(8,128)(2,1)} %get-tuple-element.7) | copy-start | bytes 3145732
  153.1 3.4 %copy-start = (f32[128,3072]{1,0:T(8,128)S(1)}, f32[128,3072]{1,0:T(8,128)}, u32[]{:S(2)}) copy-start(f32[128,3072]{1,0:T(8,128)} %get-tuple-element.14) | copy-start | bytes 4718596

commit v5 on v4

--- a/solution.py
+++ b/solution.py
@@ -213,21 +213,18 @@
 
 OFFSET, SPAN, PROJECT_ROWS = 9, 1, 512
 STEPS = 8
-KINDS = ("a1u", "a1d", "bx", "a2u", "a2d", "b1u", "b1d", "ax", "b2u", "b2d", "p1", "r0", "r1", "r2", "g0", "g1", "g2", "pb", "ma", "mb")
+KINDS = ("a1u", "a1d", "bx", "a2u", "a2d", "b1u", "b1d", "ax", "b2u", "b2d")
 
 
 def sample_and_pair(t):
-    if isinstance(t, int):
-        return (t // 2, t % 2) if t < 4 else (t % 2, t // 2)
-    early = t < 4
-    return jnp.where(early, t // 2, t % 2), jnp.where(early, t % 2, t // 2)
+    return t // 4, t % 4
 
 
 def main_kernel(cycle_ref, cross_ref, lat_hbm, w_hbm, g_hbm, att_full, dw_out, dl_out,
                 lat, w, g, k_s, v_s, q_s, st, pb, gs, att, own, out, inbox, gp, dwb, dl_out_s, dl_in,
                 z1u, z1d, z2u, z2d, su, sd, zs, xin, xain, xa, q1u, q1d, q2u, q2d, qsu, qsd,
-                whole, v1, vsum, v2, fin, fing, mate_in,
-                local, tsend, trecv, rsend, rrecv, dsend, drecv, gsend, grecv):
+                whole, parts, fin, fing,
+                local, tsend, trecv, rsend, rrecv, vsend, vrecv, dsend, drecv, gsend, grecv):
     me = Place()
     c, y, z, xh, xl = me.core, me.y, me.z, me.x_hi, me.x_lo
     zu, zd, zf = (z + 1) % 4, (z + 3) % 4, (z + 2) % 4
@@ -243,7 +240,10 @@
         kept.append(pltpu.make_async_copy(g_hbm.at[s, :, at(c * width, width)], g.at[s, at(c * TOK, TOK)], local.at[14 + s]))
     for copy in strips + kept:
         copy.start()
-    greet((me.up, me.down, me.over, me.pair, me.mate, me.z_up, me.z_down, me.outer))
+    chip = me.view // 2
+    chips = [{"view": 2 * ((chip + d) % 8) + c, "fsdp": me.fsdp} for d in range(8)]
+    others = [{"view": 2 * ((chip + d) % 8) + 1 - c, "fsdp": me.fsdp} for d in range(8)]
+    greet((*chips[1:], *others, me.z_up, me.z_down, me.outer))
 
     def weight(link):
         return jnp.where(link > 0, 0.0, -1e30).astype(F32)
@@ -266,36 +266,31 @@
         return pltpu.make_async_remote_copy(
             src_ref=src, dst_ref=dst, send_sem=send, recv_sem=recv, device_id=to, device_id_type=MESH)
 
-    def up(t):
-        return mail(out.at[t % 3, 1], inbox.at[t, 1], tsend.at[0, t % 3], trecv.at[0, t], me.up)
-
-    def down(t):
-        return mail(out.at[t % 3, 0], inbox.at[t, 0], tsend.at[1, t % 3], trecv.at[1, t], me.down)
-
-    def across(t):
-        return mail(out.at[t % 3, 2], inbox.at[t, 2], tsend.at[2, t % 3], trecv.at[2, t], me.pair)
+    def up(t, i):
+        return mail(out.at[t % 3, 1, i], inbox.at[t, 1, i], tsend.at[i, t % 3], trecv.at[i, t], me.up)
+
+    def down(t, i):
+        return mail(out.at[t % 3, 0, i], inbox.at[t, 0, i], tsend.at[2 + i, t % 3], trecv.at[2 + i, t], me.down)
+
+    def across(t, i):
+        return mail(out.at[t % 3, 2, i], inbox.at[t, 2, i], tsend.at[4 + i, t % 3], trecv.at[4 + i, t], me.pair)
 
     def columns(t):
         return at(c * width + sample_and_pair(t)[1] * 128, 128)
 
     def att_mate(t):
         return mail(att.at[t % 3, at((1 - c) * TOK, TOK)], att_full.at[sample_and_pair(t)[0], :, columns(t)],
-                    tsend.at[3, t % 3], trecv.at[3, t], me.mate)
+                    tsend.at[6, t % 3], trecv.at[6, t], me.mate)
 
     def att_own(t):
         return pltpu.make_async_copy(
-            att.at[t % 3, at(c * TOK, TOK)], att_full.at[sample_and_pair(t)[0], :, columns(t)], tsend.at[4, t % 3])
+            att.at[t % 3, at(c * TOK, TOK)], att_full.at[sample_and_pair(t)[0], :, columns(t)], tsend.at[7, t % 3])
 
     def red(kind, p, src, dst, to):
         i = KINDS.index(kind)
         return mail(src, dst, rsend.at[i, p], rrecv.at[i, p], to)
 
     lo, hi, top, low = pl.ds(0, 32), pl.ds(32, 32), pl.ds(0, 64), pl.ds(64, 64)
-    hr, er = 64, 16
-    mine = at(xl * hr + y * er, er)
-    half = at(xl * hr, hr)
-    other = at((1 - xl) * hr, hr)
-
     def a1u(p):
         return red("a1u", p, dwb.at[p, :, zf, lo], z1u.at[p], me.z_up)
 
@@ -326,38 +321,46 @@
     def b2d(p):
         return red("b2d", p, qsd.at[p], q2d.at[p], me.z_down)
 
-    def p1(p):
-        return red("p1", p, whole.at[p, other], v1.at[p], me.pair)
-
-    def ring(p):
-        return [red(f"r{d}", p, vsum.at[p, at(((y + 1 + d) % 4) * er, er)], v2.at[p, d], to)
-                for d, to in enumerate((me.up, me.over, me.down))]
-
-    def back(p):
-        return [red(f"g{d}", p, fin.at[p], fing.at[p, mine], to) for d, to in enumerate((me.up, me.over, me.down))]
-
-    def pair_back(p):
-        return red("pb", p, fing.at[p, half], fing.at[p, half], me.pair)
-
-    def mate_half(p):
-        return red("ma", p, fing.at[p, half], mate_in.at[p, half], me.mate)
-
-    def mate_other(p):
-        return red("mb", p, fing.at[p, other], mate_in.at[p, other], me.mate)
+    def scatter(group):
+        return [mail(whole.at[pl.ds(2 * group, 2), at(((chip + d) % 8) * 16, 16)], parts.at[group, d - 1],
+                     vsend.at[group, d - 1], vrecv.at[group, d - 1], chips[d]) for d in range(1, 8)]
+
+    def spread(group):
+        rows = at(chip * 16, 16)
+        return [mail(fin.at[group], fing.at[c, pl.ds(2 * group, 2), rows], vsend.at[group, 7 + i], vrecv.at[group, 7 + i], to)
+                for i, to in enumerate((*chips[1:], *others))]
 
     def f32(x):
         return x.astype(F32)
 
-    def weight_grad(p):
-        for f in range(8):
-            total = None
-            for s in range(2):
-                part = dot(lat[s, pl.ds(3 * TOK, 2 * TOK), f * 128:(f + 1) * 128], gp[p, pl.ds(s * 512, 512), :], TN)
-                total = part if total is None else total + part
-            dwb[p, f // 4, f % 4] = total.astype(BF)
+    def weight_grad(t):
+        slot = t % 3
+        p = sample_and_pair(t)[1]
+
+        def share(b):
+            if b in (3, 4):
+                part = own[slot, :, :, (b - 3) * TOK:(b - 2) * TOK].astype(BF)
+            else:
+                n, w = {0: (2, 0), 1: (0, 0), 2: (0, 1), 5: (1, 0), 6: (1, 1), 7: (2, 1)}[b]
+                part = out[slot, n, :, :, w * TOK:(w + 1) * TOK]
+            return part.reshape(256, TOK)
+
+        mine = pl.ds(3 * TOK, 2 * TOK)
+        queries = gp[p, pl.ds(512, 512), :128].astype(F32).T.astype(BF)
+        sums = gp[p, pl.ds(0, 512), :].astype(F32).T.astype(BF)
+        for f in range(4):
+            cols = slice(f * 256, (f + 1) * 256)
+            earlier = dot(sums, lat[0, mine, cols])
+            total = earlier[128:]
+            for b in range(8):
+                total = total + dot(share(b), lat[1, pl.ds(b * TOK, TOK), cols])
+            for k in range(2):
+                half = slice(k * 128, (k + 1) * 128)
+                block = dwb.at[p, f // 2, 2 * (f % 2) + k]
+                block[:, :128] = (earlier[:128, half] + dot(queries, lat[1, mine, f * 256 + k * 128:f * 256 + (k + 1) * 128])).T.astype(BF)
+                block[:, 128:] = total[:, half].T.astype(BF)
 
     def phase1(p):
-        weight_grad(p)
         for make in (a1u, a1d, bx):
             make(p).start()
 
@@ -395,68 +398,59 @@
         whole[p, low] = (f32(xa[p, z]) + f32(q2u[p]) + f32(q2d[p])).astype(BF)
         ax(p).wait_recv()
         whole[p, top] = (f32(zs[p, xh]) + f32(xin[p])).astype(BF)
-        p1(p).start()
+        if p % 2:
+            for copy in scatter(p // 2):
+                copy.start()
 
     def phase5(p):
-        p1(p).wait_recv()
-        vsum[p] = (f32(whole[p, half]) + f32(v1[p])).astype(BF)
-        for copy in ring(p):
-            copy.start()
-
-    def phase6(p):
-        total = f32(vsum[p, at(y * er, er)])
-        for d, copy in enumerate(ring(p)):
-            copy.wait_recv()
-            total = total + f32(v2[p, d])
-        fin[p] = total.astype(BF)
-        fing[p, mine] = total.astype(BF)
-        for copy in back(p):
-            copy.start()
-
-    def phase7(p):
-        for copy in back(p):
-            copy.wait_recv()
-        pair_back(p).start()
-        mate_half(p).start()
-
-    def phase8(p):
-        pair_back(p).wait_recv()
-        mate_other(p).start()
-
-    phases = (phase1, phase2, phase3, phase4, phase5, phase6, phase7, phase8)
-    begins = (4, 5, 7, 9)
+        if p % 2:
+            group = p // 2
+            total = f32(whole[2 * group:2 * group + 2, at(chip * 16, 16)])
+            for d, copy in enumerate(scatter(group)):
+                copy.wait_recv()
+                total = total + f32(parts[group, d])
+            fin[group] = total.astype(BF)
+            fing[c, 2 * group:2 * group + 2, at(chip * 16, 16)] = total.astype(BF)
+            for copy in spread(group):
+                copy.start()
+
+    phases = (phase1, phase2, phase3, phase4, phase5)
+    begins = (4, 5, 6, 7)
 
     def gather_grads(t):
-        across(t).wait_recv()
+        across(t, 0).wait_recv()
+        across(t, 1).wait_recv()
         s, p = sample_and_pair(t)
         for i in range(2):
             total = own[t % 3, i] + f32(inbox[t, 2, i]) + f32(inbox[t, 1, i]) * keep_down + f32(inbox[t, 0, i]) * keep_up
             gp[p, at(s * 512, 512), (1 + i) * 128:(2 + i) * 128] = total.T.astype(BF)
 
+    def join(u, i):
+        up(u, i).wait_recv()
+        down(u, i).wait_recv()
+
+        @pl.when(first)
+        def _():
+            out[u % 3, 2, i] = (f32(out[u % 3, 2, i]) + f32(inbox[u, 1, i])).astype(BF)
+
+        @pl.when(last)
+        def _():
+            out[u % 3, 2, i] = (f32(out[u % 3, 2, i]) + f32(inbox[u, 0, i])).astype(BF)
+
+        pl.when(edge)(across(u, i).start)
+
     def service(t):
-        @when(both(t >= 1, t <= STEPS))
-        def _():
-            u = t - 1
-            up(u).wait_recv()
-            down(u).wait_recv()
-
-            @pl.when(first)
-            def _():
-                out[u % 3, 2] = (f32(out[u % 3, 2]) + f32(inbox[u, 1])).astype(BF)
-
-            @pl.when(last)
-            def _():
-                out[u % 3, 2] = (f32(out[u % 3, 2]) + f32(inbox[u, 0])).astype(BF)
-
-            @pl.when(edge)
-            def _():
-                across(u).start()
-
-        when(both(t >= 2, t <= STEPS + 1))(lambda: gather_grads(t - 2))
+        @pl.when(t >= 1)
+        def _():
+            join(t - 1, 0)
+            join(t - 1, 1)
+
         for p, begin in reversed(list(enumerate(begins))):
             for k, phase in enumerate(phases):
-                if isinstance(t, int) or begin + k < STEPS:
-                    when(t == begin + k)(functools.partial(phase, p))
+                if 0 < k and begin + k < STEPS:
+                    pl.when(t == begin + k)(functools.partial(phase, p))
+
+        pl.when(t >= 2)(lambda: gather_grads(t - 2))
 
     sent = []
     slots = iter(range(64))
@@ -471,9 +465,9 @@
         return lat.at[s, at(b * TOK + start, size)]
 
     def w_at(f, group, start=0, size=128):
-        return w.at[at(f * 128 + start, size), pl.ds(group * 768, 768)]
-
-    cuts = {0: [(i * 64, 64) for i in range(4)], 1: [(0, TOK)]}
+        return w.at[at(f * 128 + start, size), pl.ds(1152, 384) if group else pl.ds(0, 1152)]
+
+    cuts = {0: [(i * 64, 64) for i in range(4)], 1: [(0, TOK // 2), (TOK // 2, TOK // 2)]}
     to_pair, to_up, to_down, to_mate, relays, g_mate = {}, {}, {}, {}, {}, []
     for s in range(2):
         to_pair[s] = [post(lat_hbm.at[s, pl.ds(*cut)], rows_at(s, 7 * c, *cut), me.pair) for cut in cuts[s]]
@@ -496,7 +490,7 @@
     ) for grp in range(2)]
 
     def w_first(grp):
-        for copy in strips[6 * grp:6 * grp + 6]:
+        for copy in strips[9:] if grp else strips[:9]:
             copy.wait()
         for name in ("up", "down", "out"):
             w_mail[grp][name].start()
@@ -558,17 +552,20 @@
         lat_wrap(0, i)
         if i == 1:
             w_second(0)
+            to_pair[1][0].start()
         if i == 2:
             w_third(0)
     relays[0][0].start()
-    to_pair[1][0].start()
+    to_pair[1][1].start()
+    w_first(1)
     lat_relay(0)
-    w_first(1)
     lat_first(1)
+    w_second(1)
     w_last(0)
     for copy in kept:
         copy.wait()
     lat_last(0)
+    lat_wrap(1, 0)
 
     def projected(t, slot):
         for _ in project(lat, w, *sample_and_pair(t), k_s.at[slot], v_s.at[slot], q_s.at[slot]):
@@ -581,101 +578,123 @@
 
         @pl.when(t == 2)
         def _():
+            w_last(1)
+
+        @pl.when(t == 4)
+        def _():
             lat_last(1)
-            projected(2, 0)
-
-        @pl.when(t == 3)
-        def _():
-            w_last(1)
+            projected(4, 0)
 
         @pl.when(t >= 3)
         def _():
             u = t - 3
-            up(u).wait_send()
-            down(u).wait_send()
-            across(u).wait_send()
+            for i in range(2):
+                up(u, i).wait_send()
+                down(u, i).wait_send()
+                across(u, i).wait_send()
             att_mate(u).wait_send()
             att_own(u).wait()
 
         now, later = t % 2, (t + 1) % 2
-        s_next, p_next = sample_and_pair(jnp.where(t == 1, 1, jnp.minimum(t + 1, STEPS - 1)))
+        s_next, p_next = sample_and_pair(jnp.where(t == 3, 3, jnp.minimum(t + 1, STEPS - 1)))
         beside = project(lat, w, s_next, p_next, k_s.at[later], v_s.at[later], q_s.at[later])
         attend(bias, s, p, g, k_s.at[now], v_s.at[now], q_s.at[now], st, pb, gs, att.at[t % 3],
                gp.at[p, at(s * 512, 512), pl.ds(0, 128)], own.at[t % 3], out.at[t % 3], [(4, 2, beside)])
-        up(t).start()
-        down(t).start()
-
-        @pl.when(jnp.logical_not(edge))
-        def _():
-            across(t).start()
-
+        def send(i):
+            up(t, i).start()
+            down(t, i).start()
+            pl.when(jnp.logical_not(edge))(across(t, i).start)
+
+        send(0)
         att_mate(t).start()
         att_own(t).start()
 
+        @pl.when(t >= 4)
+        def _():
+            weight_grad(t)
+            phase1(t - 4)
+
+        send(1)
+
         @pl.when(t == 0)
         def _():
-            lat_wrap(1, 0)
+            lat_wrap(1, 1)
             relays[1][0].start()
-            w_second(1)
-
-        @pl.when(t == 1)
+            w_third(1)
+
+        @pl.when(t == 2)
         def _():
             lat_relay(1)
-            w_third(1)
 
         service(t)
         return carry
 
     lax.fori_loop(0, STEPS, step, 0)
 
-    def latent_grad():
+    def latent_grad(pairs):
         for n in range(4):
-            w_n = w[pl.ds(n * 256, 256), :]
             for r in range(4):
                 rows = pl.ds(r * 256, 256)
-                total = None
-                for p in range(4):
-                    part = dot(gp[p, rows, :], w_n[:, p * 384:(p + 1) * 384], NT)
+                total = None if pairs[0] == 0 else st[n // 2, n % 2, rows, :]
+                for p in pairs:
+                    part = dot(gp[p, rows, :], w[pl.ds(n * 256, 256), p * 384:(p + 1) * 384], NT)
                     total = part if total is None else total + part
                 st[n // 2, n % 2, rows, :] = total
 
     def dl_mate():
         return mail(dl_out_s, dl_in, dsend.at[0], drecv.at[0], me.mate)
 
-    service(STEPS)
-    service(STEPS + 1)
-    latent_grad()
+    def finish(group):
+        for copy in spread(group):
+            copy.wait_recv()
+        for p in (2 * group, 2 * group + 1):
+            for core in range(2):
+                for k in range(3):
+                    first_column = (2 * k + core) * width + p * 128
+                    dw_out[:, first_column:first_column + 128] = f32(fing[core, p, :, k * 128:(k + 1) * 128])
+
+    end = STEPS - 1
+    join(end, 0)
+    latent_grad((0,))
+    join(end, 1)
+    phase2(3)
+    phase3(2)
+    phase4(1)
+    gather_grads(end - 1)
+    latent_grad((1,))
+    phase3(3)
+    phase4(2)
+    phase5(1)
+    gather_grads(end)
+    latent_grad((2,))
+    phase4(3)
+    latent_grad((3,))
     for s in range(2):
         for n in range(4):
             dl_out_s[s, :, n * 256:(n + 1) * 256] = st[n // 2, n % 2, at(s * 512 + (1 - c) * TOK, TOK), :].astype(BF)
     dl_mate().start()
-    service(STEPS + 2)
-    service(STEPS + 3)
+    phase5(3)
+    finish(0)
     dl_mate().wait_recv()
     for s in range(2):
         for n in range(4):
             cols = slice(n * 256, (n + 1) * 256)
             dl_out[s, :, cols] = (st[n // 2, n % 2, at(s * 512 + c * TOK, TOK), :] + f32(dl_in[s, :, cols])).astype(BF)
-    for t in range(STEPS + 4, STEPS + 9):
-        service(t)
-    for p in range(4):
-        for k in range(3):
-            dw_out[:, at((2 * k + c) * width + p * 128, 128)] = f32(fing[p, :, k * 128:(k + 1) * 128])
-        mate_half(p).wait_recv()
-        mate_other(p).wait_recv()
-        for k in range(3):
-            dw_out[:, at((2 * k + 1 - c) * width + p * 128, 128)] = f32(mate_in[p, :, k * 128:(k + 1) * 128])
+    finish(1)
     for t in range(STEPS - 3, STEPS):
-        for make in (up, down, across, att_mate):
-            make(t).wait_send()
+        for make in (up, down, across):
+            make(t, 0).wait_send()
+            make(t, 1).wait_send()
+        att_mate(t).wait_send()
         att_own(t).wait()
     for t in range(STEPS):
         att_mate(t).wait_recv()
     dl_mate().wait_send()
     for p in range(4):
-        for make in (a1u, a1d, bx, a2u, a2d, b1u, b1d, ax, b2u, b2d, p1, pair_back, mate_half, mate_other):
+        for make in (a1u, a1d, bx, a2u, a2d, b1u, b1d, ax, b2u, b2d):
             make(p).wait_send()
-        for copy in ring(p) + back(p):
+    for group in range(2):
+        for copy in scatter(group) + spread(group):
             copy.wait_send()
     for i, copy in enumerate(sent):
         if i >= chunks:
@@ -696,7 +715,7 @@
     att_full, dw_out, dl_out = pl.pallas_call(
         main_kernel,
         in_specs=[SM, SM, ANY, ANY, ANY],
-        out_specs=[ANY, VM, VM],
+        out_specs=[VM, VM, VM],
         out_shape=[
             jax.ShapeDtypeStruct((samples, toks, model), BF),
             jax.ShapeDtypeStruct((rows, wide), F32),
@@ -715,10 +734,11 @@
             vm(4, 64, W), vm(4, 4, 64, W), vm(4, 4, 64, W),
             vm(4, 32, W), vm(4, 32, W),
             vm(4, 64, W), vm(4, 64, W), vm(4, 64, W), vm(4, 64, W),
-            vm(4, rows, W), vm(4, 64, W), vm(4, 64, W), vm(4, 3, 16, W), vm(4, 16, W), vm(4, rows, W), vm(4, rows, W),
+            vm(4, rows, W), vm(2, 7, 2, 16, W), vm(2, 2, 16, W), vm(2, 4, rows, W),
             pltpu.SemaphoreType.DMA((16,)),
-            pltpu.SemaphoreType.DMA((5, 3)), pltpu.SemaphoreType.DMA((4, STEPS)),
+            pltpu.SemaphoreType.DMA((8, 3)), pltpu.SemaphoreType.DMA((7, STEPS)),
             pltpu.SemaphoreType.DMA((len(KINDS), 4)), pltpu.SemaphoreType.DMA((len(KINDS), 4)),
+            pltpu.SemaphoreType.DMA((2, 22)), pltpu.SemaphoreType.DMA((2, 22)),
             pltpu.SemaphoreType.DMA((1,)), pltpu.SemaphoreType.DMA((1,)),
             pltpu.SemaphoreType.DMA((64,)), pltpu.SemaphoreType.DMA((64,)),
         ],

time: 158 us -> 143 us (0.905)
  Pallas kernels: 152 us -> 138 us
    pallas_call x1, Pallas kernels: 152 us -> 138 us  [local(): pl.pallas_call(main_kernel, in_specs=[SM, SM, ANY, ANY, ANY], out_specs=[...]
where the time goes in v5:
time: 143 us
  Pallas kernels  138 us (97%)
  local copies, waits for them, and re-layouts  4.54 us (3%)
    pallas_call x1, Pallas kernels, local(): pl.pallas_call(main_kernel, in_specs=[SM, SM, ANY, ANY, ANY], out_specs=[...  138 us
    unnamed x7, local copies, waits for them, and re-layouts  4.54 us

profile of v5, /device:TPU:1, one launch (start us, length us, event | category | flops | bytes accessed | tf_op | source)
XLA Modules:
  0.0 142.9 jit_solution(10064746298382802347)
XLA Ops:
  0.6 137.7 %shard_map.76 = (bf16[2,256,1024]{2,1,0:T(8,128)(2,1)}, f32[128,3072]{1,0:T(8,128)}, bf16[2,256,1024]{2,1,0:T(8,128)(2,1)}) custom-call(s32[16]{0:T(128)} %bitcast.10, s32[8]{0:T(128)} %bitcast.11, bf16[2,256,1024]{2,1,0:T(8,128)(2,1)} %bitcast.6, bf16[128,3072]{1,0:T(8,128)(2,1)} %w_hbm.1, bf16[2,256,1024]{2,1,0:T(8,128)(2,1)} %bitcast.7), custom_call_target="tpu_custom_call" | custom-call | tf_op jit(solution)/shard_map/pallas_call | solution.py:715
  138.3 0.0 copy-start.1
  138.3 0.0 copy-start
  138.3 2.4 %copy.11 = bf16[1,1,2,256,1024]{4,3,2,1,0:T(8,128)(2,1)} copy(bf16[1,1,2,256,1024]{4,3,2,1,0:T(8,128)(2,1)} %bitcast.9) | data formatting | bytes 2097152
  140.8 0.0 copy-done.1
  140.8 1.0 copy.12
  141.7 0.0 copy-done
  141.7 1.1 copy.13
Async XLA Ops:
  138.3 2.4 %copy-start.1 = (bf16[2,256,1024]{2,1,0:T(8,128)(2,1)S(1)}, bf16[2,256,1024]{2,1,0:T(8,128)(2,1)}, u32[]{:S(2)}) copy-start(bf16[2,256,1024]{2,1,0:T(8,128)(2,1)} %get-tuple-element.7) | copy-start | bytes 3145732
  138.3 3.4 %copy-start = (f32[128,3072]{1,0:T(8,128)S(1)}, f32[128,3072]{1,0:T(8,128)}, u32[]{:S(2)}) copy-start(f32[128,3072]{1,0:T(8,128)} %get-tuple-element.14) | copy-start | bytes 4718596

commit v6 on v5

--- a/solution.py
+++ b/solution.py
@@ -211,8 +211,8 @@
         dq[rows, :] = jnp.concatenate([dq_t[0], dq_t[1]], axis=0).T.astype(BF)
 
 
-OFFSET, SPAN, PROJECT_ROWS = 9, 1, 512
-STEPS = 8
+OFFSET, SPAN, PROJECT_ROWS = 10, 1, 512
+STEPS, SLOTS = 8, 4
 KINDS = ("a1u", "a1d", "bx", "a2u", "a2d", "b1u", "b1d", "ax", "b2u", "b2d")
 
 
@@ -267,24 +267,24 @@
             src_ref=src, dst_ref=dst, send_sem=send, recv_sem=recv, device_id=to, device_id_type=MESH)
 
     def up(t, i):
-        return mail(out.at[t % 3, 1, i], inbox.at[t, 1, i], tsend.at[i, t % 3], trecv.at[i, t], me.up)
+        return mail(out.at[t % SLOTS, 1, i], inbox.at[t, 1, i], tsend.at[i, t % SLOTS], trecv.at[i, t], me.up)
 
     def down(t, i):
-        return mail(out.at[t % 3, 0, i], inbox.at[t, 0, i], tsend.at[2 + i, t % 3], trecv.at[2 + i, t], me.down)
+        return mail(out.at[t % SLOTS, 0, i], inbox.at[t, 0, i], tsend.at[2 + i, t % SLOTS], trecv.at[2 + i, t], me.down)
 
     def across(t, i):
-        return mail(out.at[t % 3, 2, i], inbox.at[t, 2, i], tsend.at[4 + i, t % 3], trecv.at[4 + i, t], me.pair)
+        return mail(out.at[t % SLOTS, 2, i], inbox.at[t, 2, i], tsend.at[4 + i, t % SLOTS], trecv.at[4 + i, t], me.pair)
 
     def columns(t):
         return at(c * width + sample_and_pair(t)[1] * 128, 128)
 
     def att_mate(t):
-        return mail(att.at[t % 3, at((1 - c) * TOK, TOK)], att_full.at[sample_and_pair(t)[0], :, columns(t)],
-                    tsend.at[6, t % 3], trecv.at[6, t], me.mate)
+        return mail(att.at[t % SLOTS, at((1 - c) * TOK, TOK)], att_full.at[sample_and_pair(t)[0], :, columns(t)],
+                    tsend.at[6, t % SLOTS], trecv.at[6, t], me.mate)
 
     def att_own(t):
         return pltpu.make_async_copy(
-            att.at[t % 3, at(c * TOK, TOK)], att_full.at[sample_and_pair(t)[0], :, columns(t)], tsend.at[7, t % 3])
+            att.at[t % SLOTS, at(c * TOK, TOK)], att_full.at[sample_and_pair(t)[0], :, columns(t)], tsend.at[7, t % SLOTS])
 
     def red(kind, p, src, dst, to):
         i = KINDS.index(kind)
@@ -334,7 +334,7 @@
         return x.astype(F32)
 
     def weight_grad(t):
-        slot = t % 3
+        slot = t % SLOTS
         p = sample_and_pair(t)[1]
 
         def share(b):
@@ -414,15 +414,13 @@
             for copy in spread(group):
                 copy.start()
 
-    phases = (phase1, phase2, phase3, phase4, phase5)
-    begins = (4, 5, 6, 7)
 
     def gather_grads(t):
         across(t, 0).wait_recv()
         across(t, 1).wait_recv()
         s, p = sample_and_pair(t)
         for i in range(2):
-            total = own[t % 3, i] + f32(inbox[t, 2, i]) + f32(inbox[t, 1, i]) * keep_down + f32(inbox[t, 0, i]) * keep_up
+            total = own[t % SLOTS, i] + f32(inbox[t, 2, i]) + f32(inbox[t, 1, i]) * keep_down + f32(inbox[t, 0, i]) * keep_up
             gp[p, at(s * 512, 512), (1 + i) * 128:(2 + i) * 128] = total.T.astype(BF)
 
     def join(u, i):
@@ -431,26 +429,31 @@
 
         @pl.when(first)
         def _():
-            out[u % 3, 2, i] = (f32(out[u % 3, 2, i]) + f32(inbox[u, 1, i])).astype(BF)
+            out[u % SLOTS, 2, i] = (f32(out[u % SLOTS, 2, i]) + f32(inbox[u, 1, i])).astype(BF)
 
         @pl.when(last)
         def _():
-            out[u % 3, 2, i] = (f32(out[u % 3, 2, i]) + f32(inbox[u, 0, i])).astype(BF)
+            out[u % SLOTS, 2, i] = (f32(out[u % SLOTS, 2, i]) + f32(inbox[u, 0, i])).astype(BF)
 
         pl.when(edge)(across(u, i).start)
 
     def service(t):
-        @pl.when(t >= 1)
-        def _():
-            join(t - 1, 0)
-            join(t - 1, 1)
-
-        for p, begin in reversed(list(enumerate(begins))):
-            for k, phase in enumerate(phases):
-                if 0 < k and begin + k < STEPS:
-                    pl.when(t == begin + k)(functools.partial(phase, p))
-
-        pl.when(t >= 2)(lambda: gather_grads(t - 2))
+        def joins(first_step, count=1):
+            for u in range(count):
+                join(first_step + u, 0)
+                join(first_step + u, 1)
+
+        pl.when(both(t >= 2, t <= 4))(lambda: joins(t - 2))
+        pl.when(t == 4)(lambda: joins(3))
+        pl.when(t >= 5)(lambda: joins(t - 1))
+
+        pl.when(t == 6)(lambda: phase2(0))
+        pl.when(t == 7)(lambda: phase2(1))
+        pl.when(t == 7)(lambda: phase3(0))
+
+        pl.when(both(t >= 3, t <= 5))(lambda: gather_grads(t - 3))
+        pl.when(t == 5)(lambda: gather_grads(3))
+        pl.when(t >= 6)(lambda: gather_grads(t - 2))
 
     sent = []
     slots = iter(range(64))
@@ -585,9 +588,9 @@
             lat_last(1)
             projected(4, 0)
 
-        @pl.when(t >= 3)
+        @pl.when(t >= SLOTS)
         def _():
-            u = t - 3
+            u = t - SLOTS
             for i in range(2):
                 up(u, i).wait_send()
                 down(u, i).wait_send()
@@ -598,8 +601,8 @@
         now, later = t % 2, (t + 1) % 2
         s_next, p_next = sample_and_pair(jnp.where(t == 3, 3, jnp.minimum(t + 1, STEPS - 1)))
         beside = project(lat, w, s_next, p_next, k_s.at[later], v_s.at[later], q_s.at[later])
-        attend(bias, s, p, g, k_s.at[now], v_s.at[now], q_s.at[now], st, pb, gs, att.at[t % 3],
-               gp.at[p, at(s * 512, 512), pl.ds(0, 128)], own.at[t % 3], out.at[t % 3], [(4, 2, beside)])
+        attend(bias, s, p, g, k_s.at[now], v_s.at[now], q_s.at[now], st, pb, gs, att.at[t % SLOTS],
+               gp.at[p, at(s * 512, 512), pl.ds(0, 128)], own.at[t % SLOTS], out.at[t % SLOTS], [(4, 2, beside)])
         def send(i):
             up(t, i).start()
             down(t, i).start()
@@ -655,6 +658,9 @@
 
     end = STEPS - 1
     join(end, 0)
+    phase2(2)
+    phase3(1)
+    phase4(0)
     latent_grad((0,))
     join(end, 1)
     phase2(3)
@@ -665,9 +671,9 @@
     phase3(3)
     phase4(2)
     phase5(1)
-    gather_grads(end)
     latent_grad((2,))
     phase4(3)
+    gather_grads(end)
     latent_grad((3,))
     for s in range(2):
         for n in range(4):
@@ -681,7 +687,7 @@
             cols = slice(n * 256, (n + 1) * 256)
             dl_out[s, :, cols] = (st[n // 2, n % 2, at(s * 512 + c * TOK, TOK), :] + f32(dl_in[s, :, cols])).astype(BF)
     finish(1)
-    for t in range(STEPS - 3, STEPS):
+    for t in range(STEPS - SLOTS, STEPS):
         for make in (up, down, across):
             make(t, 0).wait_send()
             make(t, 1).wait_send()
@@ -701,6 +707,31 @@
             copy.wait_send()
 
 
+def hand_over_kernel(*refs):
+    ins, outs, held, sems = refs[:3], refs[3:6], refs[6:9], refs[9]
+    loads = [pltpu.make_async_copy(ins[i], held[i], sems.at[0, i]) for i in range(3)]
+    stores = [pltpu.make_async_copy(held[i], outs[i], sems.at[1, i]) for i in range(3)]
+    for load in loads:
+        load.start()
+    for load, store in zip(loads, stores):
+        load.wait()
+        store.start()
+    for store in stores:
+        store.wait()
+
+
+def hand_over(arrays):
+    ANY = pl.BlockSpec(memory_space=pl.ANY)
+    return pl.pallas_call(
+        hand_over_kernel,
+        in_specs=[ANY] * 3,
+        out_specs=[ANY] * 3,
+        out_shape=[jax.ShapeDtypeStruct(a.shape, a.dtype) for a in arrays],
+        scratch_shapes=[*[pltpu.VMEM(a.shape, a.dtype) for a in arrays], pltpu.SemaphoreType.DMA((2, 3))],
+        compiler_params=pltpu.CompilerParams(vmem_limit_bytes=VMEM_LIMIT),
+    )(*arrays)
+
+
 def local(latents, w_qkv, cycle_links, cross_links, d_attended):
     _, _, samples, toks, model = latents.shape
     rows, wide = w_qkv.shape
@@ -725,8 +756,8 @@
             vm(samples, 8 * toks, model), vm(model, wide // 2), vm(samples, 2 * toks, half),
             vm(2, 8 * toks, 128), vm(2, 8 * toks, 128), vm(2, 2 * toks, 128),
             vm(2, 2, 6 * toks, toks, dtype=F32), vm(2, 6 * toks, 2 * toks), vm(2, 6 * toks, 2 * toks),
-            vm(3, 2 * toks, 128), vm(3, 2, 128, 2 * toks, dtype=F32),
-            vm(3, 3, 2, 128, 2 * toks), vm(STEPS, 3, 2, 128, 2 * toks),
+            vm(SLOTS, 2 * toks, 128), vm(SLOTS, 2, 128, 2 * toks, dtype=F32),
+            vm(SLOTS, 3, 2, 128, 2 * toks), vm(STEPS, 3, 2, 128, 2 * toks),
             vm(4, samples * 2 * toks, W), vm(4, 2, 4, rows, W),
             vm(samples, toks, model), vm(samples, toks, model),
             vm(4, 2, 32, W), vm(4, 2, 32, W),
@@ -736,7 +767,7 @@
             vm(4, 64, W), vm(4, 64, W), vm(4, 64, W), vm(4, 64, W),
             vm(4, rows, W), vm(2, 7, 2, 16, W), vm(2, 2, 16, W), vm(2, 4, rows, W),
             pltpu.SemaphoreType.DMA((16,)),
-            pltpu.SemaphoreType.DMA((8, 3)), pltpu.SemaphoreType.DMA((7, STEPS)),
+            pltpu.SemaphoreType.DMA((8, SLOTS)), pltpu.SemaphoreType.DMA((7, STEPS)),
             pltpu.SemaphoreType.DMA((len(KINDS), 4)), pltpu.SemaphoreType.DMA((len(KINDS), 4)),
             pltpu.SemaphoreType.DMA((2, 22)), pltpu.SemaphoreType.DMA((2, 22)),
             pltpu.SemaphoreType.DMA((1,)), pltpu.SemaphoreType.DMA((1,)),
@@ -744,6 +775,7 @@
         ],
         compiler_params=pltpu.CompilerParams(collective_id=0, has_side_effects=True, vmem_limit_bytes=63 * 2**20),
     )(cycle_links[0], cross_links[0], latents[0, 0], w_qkv, d_attended[0, 0])
+    att_full, dl_out, dw_out = hand_over((att_full, dl_out, dw_out))
     return att_full[None, None], dl_out[None, None], dw_out
 
 

time: 143 us -> 142 us (level)
  local copies, waits for them, and re-layouts: 4.54 us -> 0 us
  Pallas kernels: 138 us -> 141 us
    unnamed x7 -> x0, local copies, waits for them, and re-layouts: 4.54 us -> none
    pallas_call x0 -> x1, Pallas kernels: none -> 3.24 us  [hand_over(): pl.pallas_call(hand_over_kernel, in_specs=[ANY] * 3, out_specs=[ANY] * 3,...]
where the time goes in v6:
time: 142 us; the launch traced here: 141 us
  Pallas kernels  141 us (99%)
    pallas_call x1, Pallas kernels, local(): pl.pallas_call(main_kernel, in_specs=[SM, SM, ANY, ANY, ANY], out_specs=[...  137 us
    pallas_call x1, Pallas kernels, hand_over(): pl.pallas_call(hand_over_kernel, in_specs=[ANY] * 3, out_specs=[ANY] * 3,...  3.24 us

profile of v6, /device:TPU:1, one launch (start us, length us, event | category | flops | bytes accessed | tf_op | source)
XLA Modules:
  0.0 141.4 jit_solution(3008241686864689038)
XLA Ops:
  0.6 137.4 %shard_map.76 = (bf16[2,256,1024]{2,1,0:T(8,128)(2,1)}, f32[128,3072]{1,0:T(8,128)}, bf16[2,256,1024]{2,1,0:T(8,128)(2,1)}) custom-call(s32[16]{0:T(128)} %bitcast.8, s32[8]{0:T(128)} %bitcast.9, bf16[2,256,1024]{2,1,0:T(8,128)(2,1)} %bitcast.6, bf16[128,3072]{1,0:T(8,128)(2,1)} %w_hbm.1, bf16[2,256,1024]{2,1,0:T(8,128)(2,1)} %bitcast.7), custom_call_target="tpu_custom_call" | custom-call | tf_op jit(solution)/shard_map/pallas_call | solution.py:746
  138.0 3.2 %shard_map.77 = (bf16[2,256,1024]{2,1,0:T(8,128)(2,1)}, bf16[2,256,1024]{2,1,0:T(8,128)(2,1)}, f32[128,3072]{1,0:T(8,128)}) custom-call(bf16[2,256,1024]{2,1,0:T(8,128)(2,1)} %get-tuple-element.9.refs_0_, bf16[2,256,1024]{2,1,0:T(8,128)(2,1)} %get-tuple-element.10.refs_1_, f32[128,3072]{1,0:T(8,128)} %get-tuple-element.11.refs_2_), custom_call_target="tpu_custom_call" | custom-call | tf_op jit(solution)/shard_map/pallas_call | solution.py:725

commit v7 on v6

--- a/solution.py
+++ b/solution.py
@@ -399,8 +399,9 @@
         ax(p).wait_recv()
         whole[p, top] = (f32(zs[p, xh]) + f32(xin[p])).astype(BF)
         if p % 2:
-            for copy in scatter(p // 2):
-                copy.start()
+            copies = scatter(p // 2)
+            for i in (5, 1, 2, 4, 6, 0, 3):
+                copies[i].start()
 
     def phase5(p):
         if p % 2:
@@ -411,8 +412,9 @@
                 total = total + f32(parts[group, d])
             fin[group] = total.astype(BF)
             fing[c, 2 * group:2 * group + 2, at(chip * 16, 16)] = total.astype(BF)
-            for copy in spread(group):
-                copy.start()
+            copies = spread(group)
+            for i in (5, 13, 1, 9, 2, 10, 4, 12, 6, 14, 0, 8, 3, 11, 7):
+                copies[i].start()
 
 
     def gather_grads(t):

time: 142 us -> 141 us (level)
  no operation moved by 1% of the time
where the time goes in v7:
time: 141 us
  Pallas kernels  140 us (99%)
    pallas_call x1, Pallas kernels, local(): pl.pallas_call(main_kernel, in_specs=[SM, SM, ANY, ANY, ANY], out_specs=[...  137 us
    pallas_call x1, Pallas kernels, hand_over(): pl.pallas_call(hand_over_kernel, in_specs=[ANY] * 3, out_specs=[ANY] * 3,...  3.24 us

profile of v7, /device:TPU:1, one launch (start us, length us, event | category | flops | bytes accessed | tf_op | source)
XLA Modules:
  0.0 140.9 jit_solution(962642061809550057)
XLA Ops:
  0.6 136.8 %shard_map.76 = (bf16[2,256,1024]{2,1,0:T(8,128)(2,1)}, f32[128,3072]{1,0:T(8,128)}, bf16[2,256,1024]{2,1,0:T(8,128)(2,1)}) custom-call(s32[16]{0:T(128)} %bitcast.8, s32[8]{0:T(128)} %bitcast.9, bf16[2,256,1024]{2,1,0:T(8,128)(2,1)} %bitcast.6, bf16[128,3072]{1,0:T(8,128)(2,1)} %w_hbm.1, bf16[2,256,1024]{2,1,0:T(8,128)(2,1)} %bitcast.7), custom_call_target="tpu_custom_call" | custom-call | tf_op jit(solution)/shard_map/pallas_call | solution.py:748
  137.5 3.2 %shard_map.77 = (bf16[2,256,1024]{2,1,0:T(8,128)(2,1)}, bf16[2,256,1024]{2,1,0:T(8,128)(2,1)}, f32[128,3072]{1,0:T(8,128)}) custom-call(bf16[2,256,1024]{2,1,0:T(8,128)(2,1)} %get-tuple-element.9.refs_0_, bf16[2,256,1024]{2,1,0:T(8,128)(2,1)} %get-tuple-element.10.refs_1_, f32[128,3072]{1,0:T(8,128)} %get-tuple-element.11.refs_2_), custom_call_target="tpu_custom_call" | custom-call | tf_op jit(solution)/shard_map/pallas_call | solution.py:727
